TPU v7x, 32 devices: a whole 2x2x4 slice. The times are simulated.
32 devices in a mesh: seq: 8 (over z, x), batch: 4 (over y, core).
Axes of the slice: x: 2, y: 2, z: 4, core: 2. Of those that a mesh axis runs over, the one named last changes fastest.
Arguments:
- tokens: bfloat16 [8, 2048, 1024], P('batch', 'seq'), may hold values from -6 to 6
- cotangent: bfloat16 [8, 2048, 1024], P('batch', 'seq'), may hold values from -6 to 6
- lengths: int32 [8], P('batch'), may hold values from 128 to 2048, as said below
- span_order: int32 [8, 2], replicated, may hold values from 0 to 15, as said below
- attn_gain: bfloat16 [1024], P('seq'), may hold values from 0.5 to 1.5
- query_heads: bfloat16 [1024, 96], P('seq'), may hold values from -0.375 to 0.375
- query_dims: bfloat16 [1024, 384], P('seq'), may hold values from -0.375 to 0.375
- key_heads: bfloat16 [1024, 32], P('seq'), may hold values from -0.25 to 0.25
- key_dims: bfloat16 [1024, 128], P('seq'), may hold values from -0.1875 to 0.1875
- value_heads: bfloat16 [1024, 32], P('seq'), may hold values from -0.375 to 0.375
- value_dims: bfloat16 [1024, 128], P('seq'), may hold values from -0.1875 to 0.1875
- out_proj: bfloat16 [1024, 1024], P('seq'), may hold values from -1.5 to 1.5
- ffn_gain: bfloat16 [1024], P('seq'), may hold values from 0.5 to 1.5
- gate_proj: bfloat16 [1024, 2816], P('seq'), may hold values from -0.1875 to 0.1875
- up_proj: bfloat16 [1024, 2816], P('seq'), may hold values from -0.1875 to 0.1875
- down_proj: bfloat16 [2816, 1024], P('seq'), may hold values from -0.109375 to 0.109375
Outputs:
- output: bfloat16 [8, 2048, 1024], P('batch', 'seq')
- input_grad: float32 [8, 2048, 1024], P('batch', 'seq')
- attn_gain_grad: float32 [1024], P('seq')
- query_heads_grad: float32 [1024, 96], P('seq')
- query_dims_grad: float32 [1024, 384], P('seq')
- key_heads_grad: float32 [1024, 32], P('seq')
- key_dims_grad: float32 [1024, 128], P('seq')
- value_heads_grad: float32 [1024, 32], P('seq')
- value_dims_grad: float32 [1024, 128], P('seq')
- out_proj_grad: float32 [1024, 1024], P('seq')
- ffn_gain_grad: float32 [1024], P('seq')
- gate_proj_grad: float32 [1024, 2816], P('seq')
- up_proj_grad: float32 [1024, 2816], P('seq')
- down_proj_grad: float32 [2816, 1024], P('seq')
Inputs may be any that keep to these rules, and one draw needn't show every extreme that they name: `lengths`: in each aligned block of 2 rows (the rows of one index of batch) at least one row has length 2048. `span_order`: the two entries of each row add up to 15 and the first is the smaller; every span number appears once.
All inputs are finite; a program needn't handle non-finite values.
Results may differ from a plain program's by a relative error of at most 0.017.
The roundings to bfloat16 on the way count: a program that leaves them out, or rounds other values in their place, can miss the bound.
Values may be sent and summed in bfloat16 or wider, within the bound.
A program may use at most 320 MiB of HBM per device.

v0:
```python
import functools
import math

import jax
import jax.numpy as jnp
from jax import lax
from jax.experimental import pallas as pl
from jax.experimental.pallas import tpu as pltpu
from jax.sharding import PartitionSpec as P


MESH = pl.DeviceIdType.MESH
NZ, NX = 4, 2

class Place:
    def __init__(self):
        self.seq = lax.axis_index("seq")
        self.batch = lax.axis_index("batch")
        self.z = self.seq // 2
        self.x = lax.rem(self.seq, 2)
        self.y = self.batch // 2
        self.c = lax.rem(self.batch, 2)
        self.up = (jnp.minimum(self.seq + 2, 7), self.batch)
        self.down = (jnp.maximum(self.seq - 2, 0), self.batch)
        self.xp = (self.seq + 1 - 2 * self.x, self.batch)
        self.yp = (self.seq, lax.rem(self.batch + 2, 4))
        self.cp = (self.seq, self.batch + 1 - 2 * self.c)

    def along(self, k):
        return (2 * lax.rem(self.z + k, NZ) + self.x, self.batch)

def greet(me):
    bar = pltpu.get_barrier_semaphore()
    def sig(d):
        pl.semaphore_signal(bar, inc=1, device_id=d, device_id_type=MESH)
    for k in range(1, NZ):
        sig(me.along(k))
    sig(me.xp); sig(me.yp); sig(me.cp)
    pl.semaphore_wait(bar, NZ + 2)

class Unit:
    def __init__(self, arr, row, col, flow, axis):
        self.arr, self.row, self.col, self.flow, self.axis = arr, row, col, flow, axis
        self.shape = (row[1], col[1])
        h = list(self.shape); h[axis] //= 2
        self.half = tuple(h)
        q = list(h)
        if flow == "P": q[axis] //= 2
        self.piece = tuple(q)

def rect(unit, ref, part, nparts):
    start = [unit.row[0], unit.col[0]]
    size = list(unit.shape)
    size[unit.axis] //= nparts
    idx = []
    for d in range(2):
        if d == unit.axis:
            off = part * size[d] + start[d]
            idx.append(pl.ds(pl.multiple_of(off, 16 if d == 0 else 128), size[d]))
        else:
            idx.append(pl.ds(start[d], size[d]))
    return ref.at[tuple(idx)]

def shard_of(ref, s, n=8):
    if len(ref.shape) == 3:
        return ref.at[s]
    rows = ref.shape[0] // n
    return ref.at[pl.ds(pl.multiple_of(s * rows, 16), rows)]

class Reduce:
    def __init__(self, me, units, ins, outs, scratch):
        self.me, self.units, self.ins, self.outs = me, units, ins, outs
        nu = len(units)
        self.A, self.RC, self.RY, self.RX, self.RZ, self.RF = [scratch[i * nu:(i + 1) * nu] for i in range(6)]
        self.ls, self.cs, self.cr, self.ys, self.yr, self.xs, self.xr, self.zs, self.zr, self.fs, self.fr, self.os_ = scratch[6 * nu:]

    def shard_at(self, i):
        me = self.me
        zz = lax.rem(me.z + 1 + lax.rem(i, NZ), NZ)
        xx = jnp.where(i < NZ, 1 - me.x, me.x)
        return zz, xx, 2 * zz + xx

    def sub(self, u, ref, y):
        if u.flow == "R":
            return ref
        n = u.piece[u.axis]
        idx = [slice(None)] * 2
        idx[u.axis] = pl.ds(pl.multiple_of(y * n, n), n)
        return ref.at[tuple(idx)]

    def remote(self, src, dst, ss, rs, dev):
        return pltpu.make_async_remote_copy(src_ref=src, dst_ref=dst, send_sem=ss, recv_sem=rs, device_id=dev, device_id_type=MESH)

    def core_copy(self, k, i):
        u = self.units[k]; zz, xx, s = self.shard_at(i)
        return self.remote(rect(u, shard_of(self.ins[u.arr], s), 1 - self.me.c, 2), self.RC[k].at[s], self.cs.at[k, s], self.cr.at[k, s], self.me.cp)

    def local_copy(self, k, i):
        u = self.units[k]; zz, xx, s = self.shard_at(i)
        return pltpu.make_async_copy(rect(u, shard_of(self.ins[u.arr], s), self.me.c, 2), self.A[k].at[s], self.ls.at[k, s])

    def y_copy(self, k, i):
        u = self.units[k]; zz, xx, s = self.shard_at(i)
        return self.remote(self.sub(u, self.A[k].at[s], 1 - self.me.y), self.RY[k].at[s], self.ys.at[k, s], self.yr.at[k, s], self.me.yp)

    def x_copy(self, k, zz):
        u, me = self.units[k], self.me
        return self.remote(self.sub(u, self.A[k].at[2 * zz + 1 - me.x], me.y), self.RX[k].at[zz], self.xs.at[k, zz], self.xr.at[k, zz], me.xp)

    def z_copy(self, k, zz):
        u, me = self.units[k], self.me
        return self.remote(self.mine(k, zz), self.RZ[k].at[self.slot(me.z, zz)], self.zs.at[k, zz], self.zr.at[k, me.z], (2 * zz + me.x, me.batch))

    @staticmethod
    def slot(source, owner):
        return lax.rem(source - owner + NZ, NZ) - 1

    def z_recv(self, k, zz):
        u, me = self.units[k], self.me
        v = self.RZ[k].at[self.slot(zz, me.z)]
        return self.remote(v, v, self.zs.at[k, zz], self.zr.at[k, zz], (2 * zz + me.x, me.batch))

    def mine(self, k, zz):
        return self.sub(self.units[k], self.A[k].at[2 * zz + self.me.x], self.me.y)

    @staticmethod
    def add(dst, src):
        dst[...] = dst[...] + src[...]

    def begin(self, k, i):
        self.core_copy(k, i).start()
        self.local_copy(k, i).start()

    def core(self, k, i):
        u = self.units[k]; zz, xx, s = self.shard_at(i)
        self.local_copy(k, i).wait()
        self.core_copy(k, i).wait_recv()
        self.add(self.A[k].at[s], self.RC[k].at[s])
        if u.flow == "P":
            self.y_copy(k, i).start()
        else:
            pl.when(i < NZ)(lambda: self.x_copy(k, zz).start())

    def y(self, k, i):
        u = self.units[k]; zz, xx, s = self.shard_at(i)
        self.y_copy(k, i).wait_recv()
        self.add(self.sub(u, self.A[k].at[s], self.me.y), self.RY[k].at[s])
        pl.when(i < NZ)(lambda: self.x_copy(k, zz).start())

    def x(self, k, i):
        me = self.me
        zz = lax.rem(me.z + 1 + i, NZ)
        self.x_copy(k, zz).wait_recv()
        self.add(self.mine(k, zz), self.RX[k].at[zz])
        pl.when(zz != me.z)(lambda: self.z_copy(k, zz).start())

    def fin_y(self, k):
        u, me = self.units[k], self.me
        mine = self.mine(k, me.z)
        dst = rect(u, self.outs[u.arr], 2 * me.c + me.y, 4) if u.flow == "P" else self.RF[k]
        return self.remote(mine, dst, self.fs.at[k, 0], self.fr.at[k, 0], me.yp)

    def fin_c(self, k, w):
        u, me = self.units[k], self.me
        if u.flow == "P":
            if w == 0:
                return self.remote(self.mine(k, me.z), rect(u, self.outs[u.arr], 2 * me.c + me.y, 4), self.fs.at[k, 1], self.fr.at[k, 1], me.cp)
            v = rect(u, self.outs[u.arr], 2 * me.c + 1 - me.y, 4)
            return self.remote(v, v, self.fs.at[k, 2], self.fr.at[k, 2], me.cp)
        return self.remote(self.RF[k], rect(u, self.outs[u.arr], me.c, 2), self.fs.at[k, 1], self.fr.at[k, 1], me.cp)

    def out_copy(self, k):
        u, me = self.units[k], self.me
        if u.flow == "P":
            return pltpu.make_async_copy(self.mine(k, me.z), rect(u, self.outs[u.arr], 2 * me.c + me.y, 4), self.os_.at[k])
        return pltpu.make_async_copy(self.RF[k], rect(u, self.outs[u.arr], me.c, 2), self.os_.at[k])

    def own(self, k, i):
        me = self.me
        def body(i, c):
            zz = lax.rem(me.z + i, NZ)
            self.z_recv(k, zz).wait_recv()
            self.add(self.mine(k, me.z), self.RZ[k].at[self.slot(zz, me.z)])
            return c
        lax.fori_loop(1, NZ, body, 0)
        self.fin_y(k).start()
        if self.units[k].flow == "P":
            self.out_copy(k).start()
            self.fin_c(k, 0).start()

    def last(self, k, i):
        self.fin_y(k).wait_recv()
        if self.units[k].flow == "P":
            self.fin_c(k, 1).start()
        else:
            self.add(self.RF[k], self.mine(k, self.me.z))
            self.out_copy(k).start()
            self.fin_c(k, 0).start()

    def end(self, k, i):
        me = self.me
        flow = self.units[k].flow
        for w in range(2 if flow == "P" else 1):
            self.fin_c(k, w).wait_recv()
            self.fin_c(k, w).wait_send()
        self.out_copy(k).wait()
        self.fin_y(k).wait_send()
        def body(i, c):
            self.core_copy(k, i).wait_send()
            if flow == "P": self.y_copy(k, i).wait_send()
            return c
        lax.fori_loop(0, 8, body, 0)
        def body(zz, c):
            self.x_copy(k, zz).wait_send()
            pl.when(zz != me.z)(lambda: self.z_copy(k, zz).wait_send())
            return c
        lax.fori_loop(0, NZ, body, 0)

    def run(self, plan):
        for step, k, first, n in plan:
            fn = getattr(self, step)
            if n == 1:
                fn(k, first)
            else:
                def body(i, c):
                    fn(k, i)
                    return c
                lax.fori_loop(first, first + n, body, 0)

def reduce_kernel(units, narr, plan, *refs):
    me = Place()
    greet(me)
    red = Reduce(me, units, refs[:narr], refs[narr:2 * narr], refs[2 * narr:])
    red.run(plan)

def reduce_scratch(units):
    nu = len(units)
    DMA = pltpu.SemaphoreType.DMA
    bf = jnp.bfloat16
    V = pltpu.VMEM
    return ([V((8, *u.half), bf) for u in units] + [V((8, *u.half), bf) for u in units]
        + [V((8, *u.piece) if u.flow == "P" else (16, 128), bf) for u in units] + [V((4, *u.piece), bf) for u in units]
        + [V((3, *u.piece), bf) for u in units] + [V(u.piece if u.flow == "R" else (16, 128), bf) for u in units]
        + [DMA((nu, 8))] * 5 + [DMA((nu, 4))] * 4 + [DMA((nu, 3))] * 2 + [DMA((nu,))])

def reduce_weights(arrays, units, plan, cid):
    narr = len(arrays)
    return pl.pallas_call(
        functools.partial(reduce_kernel, units, narr, plan),
        out_shape=[jax.ShapeDtypeStruct(a.shape[1:], a.dtype) for a in arrays],
        in_specs=[pl.BlockSpec(memory_space=pl.ANY)] * narr,
        out_specs=[pl.BlockSpec(memory_space=pl.ANY)] * narr,
        scratch_shapes=reduce_scratch(units),
        compiler_params=pltpu.CompilerParams(collective_id=cid, has_side_effects=True, vmem_limit_bytes=58 << 20),
        name="reduce_weights",
    )(*arrays)

F32, BF16 = jnp.float32, jnp.bfloat16
NEG = -1e30

def nn(a, b):
    return lax.dot_general(a, b, (((1,), (0,)), ((), ())), preferred_element_type=F32)

def nt(a, b):
    return lax.dot_general(a, b, (((1,), (1,)), ((), ())), preferred_element_type=F32)

def expand(heads, dims, base):
    parts = []
    for h in range(2):
        parts.append((heads[base + h:base + h + 1] * dims[0] + heads[base + 2 + h:base + 3 + h] * dims[1]) * 0.5)
    return jnp.concatenate(parts, 0)

def queries(qh, qr):
    parts = []
    for h in range(2):
        total = qh[h:h + 1] * qr[0:64]
        for r in range(1, 6):
            total = total + qh[2 * r + h:2 * r + h + 1] * qr[64 * r:64 * r + 64]
        parts.append(total)
    return jnp.concatenate(parts, 0) / 6.0

def lanes_below(shape, n):
    return lax.broadcasted_iota(jnp.int32, shape, 1) < n

def stack_heads(part):
    first = lanes_below(part.shape, 64)
    zero = jnp.zeros_like(part)
    return jnp.concatenate([jnp.where(first, part, zero), jnp.where(first, zero, part)], 0)

def unstack_heads(part):
    n = part.shape[0] // 2
    return jnp.where(lanes_below((n, 128), 64), part[:n], part[n:])

def causal_bias(n2, span):
    row = lax.broadcasted_iota(jnp.int32, (n2, span), 0) % span
    col = lax.broadcasted_iota(jnp.int32, (n2, span), 1)
    return jnp.where(col <= row, 0.0, NEG)

def pair_factors(heads, dims, cond, base, at):
    hl, hs = heads
    dl, ds = dims
    low = expand(hl, (dl[at:at + 64].astype(F32), dl[at + 64:at + 128].astype(F32)), base).astype(BF16)
    sel = expand(hs, (ds[at:at + 64].astype(F32), ds[at + 64:at + 128].astype(F32)), base)
    left = jnp.where(cond > 0.5, sel, 0.0).astype(BF16)
    right = jnp.where(cond > 0.5, 0.0, sel).astype(BF16)
    return low, jnp.concatenate([left, right], 0)

def attend_kernel(span, chunk, qh_ref, qr_ref, hl_ref, hs_ref, dl_ref, ds_ref, cond_ref, bl_ref, bs_ref, o_ref, lse_ref, s1, s2):
    pair_forward(span, chunk, pl.program_id(1), qh_ref[0, 0], qr_ref[0], hl_ref[0, 0], hs_ref[0, 0], dl_ref, ds_ref, cond_ref, bl_ref, bs_ref, o_ref, lse_ref, s1, s2)

def pair_forward(span, chunk, p, qh, qr, hl, hs, dl_ref, ds_ref, cond_ref, bl_ref, bs_ref, o_ref, lse_ref, s1, s2):
    n2 = 2 * span
    nk = dl_ref.shape[-1]
    qt = queries(qh, qr)
    q = (qt.astype(BF16).astype(F32).T * 0.125).astype(BF16)
    qlo, qhi = stack_heads(q[:span]), stack_heads(q[span:])
    qboth = jnp.concatenate([qlo, qhi], 1)
    heads = (hl, hs)
    dims = (dl_ref[0], ds_ref[0])
    cond = cond_ref[...]
    klo, ksel = pair_factors(heads, dims, cond, 0, 0)
    vlo, vsel = pair_factors(heads, dims, cond, 4, 128)
    tri = causal_bias(n2, span)
    width = min(128, chunk)
    mlo = jnp.full((n2, width), NEG, F32)
    mhi = jnp.full((n2, width), NEG, F32)
    s3 = nn(qlo, klo[:, :span]) + bl_ref[0][:, :span] + tri
    m3 = jnp.max(s3, -1, keepdims=True)
    for c in range(0, nk, chunk):
        sl = slice(c, c + chunk)
        a = nn(qhi, klo[:, sl]) + bl_ref[0][:, sl]
        s1[:, sl] = a
        b = nn(qboth, ksel[:, sl]) + bs_ref[0][:, sl]
        if c == 0:
            b = jnp.concatenate([b[:, :span] + tri, b[:, span:]], 1)
        s2[:, sl] = b
        for i in range(0, chunk, width):
            on = cond[:, c + i:c + i + width] > 0.5
            ai, bi = a[:, i:i + width], b[:, i:i + width]
            mlo = jnp.maximum(mlo, jnp.where(on, bi, NEG))
            mhi = jnp.maximum(mhi, jnp.maximum(ai, jnp.where(on, NEG, bi)))
    mlo = jnp.maximum(jnp.max(mlo, -1, keepdims=True), m3)
    mhi = jnp.max(mhi, -1, keepdims=True)
    e3 = jnp.exp(s3 - mlo)
    tlo = jnp.zeros((n2, width), F32)
    thi = jnp.zeros((n2, width), F32)
    o3 = nt(e3.astype(BF16), vlo[:, :span])
    o1 = jnp.zeros((n2, 128), F32)
    o2 = jnp.zeros((n2, 256), F32)
    for c in range(0, nk, chunk):
        sl = slice(c, c + chunk)
        on = cond[:, sl] > 0.5
        a = jnp.exp(s1[:, sl] - mhi)
        b = jnp.exp(s2[:, sl] - jnp.where(on, mlo, mhi))
        blo = jnp.where(on, b, 0.0)
        bhi = a + jnp.where(on, 0.0, b)
        for i in range(0, chunk, width):
            tlo = tlo + blo[:, i:i + width]
            thi = thi + bhi[:, i:i + width]
        o1 = o1 + nt(a.astype(BF16), vlo[:, sl])
        o2 = o2 + nt(b.astype(BF16), vsel[:, sl])
    llo = jnp.sum(tlo, -1, keepdims=True) + jnp.sum(e3, -1, keepdims=True)
    lhi = jnp.sum(thi, -1, keepdims=True)
    olo = unstack_heads((o2[:, :128] + o3) / llo)
    ohi = unstack_heads((o2[:, 128:] + o1) / lhi)
    o_ref[0] = jnp.concatenate([olo, ohi], 0).astype(BF16)
    lane = lax.broadcasted_iota(jnp.int32, (span, 128), 1)
    tlo = mlo + jnp.log(llo)
    thi = mhi + jnp.log(lhi)
    old = jnp.where(p == 0, 0.0, lse_ref[0])
    new = []
    for k, t in enumerate((tlo, thi)):
        part = old[k * span:(k + 1) * span]
        part = jnp.where(lane == 2 * p, t[:span], part)
        new.append(jnp.where(lane == 2 * p + 1, t[span:], part))
    lse_ref[0] = jnp.concatenate(new, 0)

def attend(qh, qr, hl, hs, dl, ds, cond, bl, bs):
    rows, pairs, _, nq = qh.shape
    nk = dl.shape[-1]
    span = nq // 2
    chunk = min(512, nk)
    full = lambda *s: pl.BlockSpec((1, *s), lambda b, p: (b, *([0] * len(s))))
    pairb = lambda *s: pl.BlockSpec((1, 1, *s), lambda b, p: (b, p, *([0] * len(s))))
    return pl.pallas_call(
        functools.partial(attend_kernel, span, chunk),
        grid=(rows, pairs),
        out_shape=[jax.ShapeDtypeStruct((rows, nq, pairs * 128), BF16), jax.ShapeDtypeStruct((rows, nq, 128), F32)],
        in_specs=[pairb(12, nq), full(384, nq), pairb(8, nk), pairb(8, nk), full(256, nk), full(256, nk),
                  pl.BlockSpec((1, nk), lambda b, p: (0, 0)), full(1, nk), full(1, nk)],
        out_specs=[pl.BlockSpec((1, nq, 128), lambda b, p: (b, 0, p)), full(nq, 128)],
        scratch_shapes=[pltpu.VMEM((nq, nk), F32), pltpu.VMEM((nq, nk), F32)],
        compiler_params=pltpu.CompilerParams(vmem_limit_bytes=56 << 20),
        name="attend",
    )(qh, qr, hl, hs, dl, ds, cond, bl, bs)

def attend_back_kernel(span, chunk, qh_ref, qr_ref, hl_ref, hs_ref, dl_ref, ds_ref, cond_ref, bl_ref, bs_ref, lse_ref, o_ref, g_ref,
                       dqh_ref, dqr_ref, dhl_ref, dhs_ref, ddl_ref, dds_ref):
    p = pl.program_id(1)
    @pl.when(p == 0)
    def _():
        dqr_ref[...] = jnp.zeros_like(dqr_ref)
        ddl_ref[...] = jnp.zeros_like(ddl_ref)
        dds_ref[...] = jnp.zeros_like(dds_ref)
    pair_back(span, chunk, p, qh_ref, qr_ref, Pair(hl_ref, 0, 0), Pair(hs_ref, 0, 0), dl_ref, ds_ref, cond_ref, bl_ref, bs_ref, lse_ref, o_ref[0], g_ref[0],
              dqh_ref, dqr_ref, Pair(dhl_ref, 0, 0), Pair(dhs_ref, 0, 0), ddl_ref, dds_ref)

class Pair:
    def __init__(self, ref, *at):
        self.ref, self.at = ref, at

    def all(self):
        return self.ref[self.at]

    def row(self, j, sl):
        return self.ref[(*self.at, slice(j, j + 1), sl)]

    def put(self, j, sl, value):
        self.ref[(*self.at, slice(j, j + 1), sl)] = value

def pair_back(span, chunk, p, qh_ref, qr_ref, hl, hs, dl_ref, ds_ref, cond_ref, bl_ref, bs_ref, lse_ref, o, g,
              dqh_ref, dqr_ref, dhl, dhs, ddl_ref, dds_ref):
    n2 = 2 * span
    nk = dl_ref.shape[-1]
    qh, qr = qh_ref[0, 0], qr_ref[0]
    qt = (queries(qh, qr).astype(BF16).astype(F32)) * 0.125
    q = qt.T.astype(BF16)
    qlo, qhi = stack_heads(q[:span]), stack_heads(q[span:])
    qboth = jnp.concatenate([qlo, qhi], 1)
    glo, ghi = stack_heads(g[:span]), stack_heads(g[span:])
    gboth = jnp.concatenate([glo, ghi], 1)
    gt = g.astype(F32).T
    first = lax.broadcasted_iota(jnp.int32, (128, span), 0) < 64
    def stack_lanes(part):
        return jnp.concatenate([jnp.where(first, part, 0.0), jnp.where(first, 0.0, part)], 1).astype(BF16)
    qtlo, qthi = stack_lanes(qt[:, :span]), stack_lanes(qt[:, span:])
    gtlo, gthi = stack_lanes(gt[:, :span]), stack_lanes(gt[:, span:])
    qtboth = jnp.concatenate([qtlo, qthi], 0)
    gtboth = jnp.concatenate([gtlo, gthi], 0)
    prod = g.astype(F32) * o.astype(F32)
    flane = lanes_below((n2, 128), 64)
    d0 = jnp.sum(jnp.where(flane, prod, 0.0), -1, keepdims=True)
    d1 = jnp.sum(jnp.where(flane, 0.0, prod), -1, keepdims=True)
    lane = lax.broadcasted_iota(jnp.int32, (n2, 128), 1)
    lse = lse_ref[0]
    l0 = jnp.sum(jnp.where(lane == 2 * p, lse, 0.0), -1, keepdims=True)
    l1 = jnp.sum(jnp.where(lane == 2 * p + 1, lse, 0.0), -1, keepdims=True)
    dello, delhi = jnp.concatenate([d0[:span], d1[:span]], 0), jnp.concatenate([d0[span:], d1[span:]], 0)
    lselo, lsehi = jnp.concatenate([l0[:span], l1[:span]], 0), jnp.concatenate([l0[span:], l1[span:]], 0)
    heads = (hl.all(), hs.all())
    dims = (dl_ref[0], ds_ref[0])
    cond = cond_ref[...]
    klo, ksel = pair_factors(heads, dims, cond, 0, 0)
    vlo, vsel = pair_factors(heads, dims, cond, 4, 128)
    tri = causal_bias(n2, span)

    def put(dkt, h, d_ref, hd, dd_ref, base, at, sl):
        for r in range(2):
            dim = d_ref[0, at + 64 * r:at + 64 * r + 64, sl].astype(F32)
            total = None
            for k in range(2):
                part = dkt[64 * k:64 * k + 64]
                j = base + 2 * r + k
                hd.put(j, sl, jnp.sum(part * dim, 0, keepdims=True) * 0.5)
                term = part * h.row(j, sl)
                total = term if total is None else total + term
            dd_ref[0, at + 64 * r:at + 64 * r + 64, sl] += total * 0.5

    s3 = nn(qlo, klo[:, :span]) + bl_ref[0][:, :span] + tri
    p3 = jnp.exp(s3 - lselo)
    dp3 = nn(glo, vlo[:, :span])
    ds3 = (p3 * (dp3 - dello)).astype(BF16)
    p3 = p3.astype(BF16)
    dq3 = nt(ds3, klo[:, :span])
    dk3 = nn(qtlo, ds3)
    dv3 = nn(gtlo, p3)
    dq1 = jnp.zeros((n2, 128), F32)
    dq2 = jnp.zeros((n2, 256), F32)
    for c in range(0, nk, chunk):
        sl = slice(c, c + chunk)
        pa = jnp.exp(nn(qhi, klo[:, sl]) + bl_ref[0][:, sl] - lsehi)
        dpa = nn(ghi, vlo[:, sl])
        dsa = (pa * (dpa - delhi)).astype(BF16)
        pa = pa.astype(BF16)
        dq1 = dq1 + nt(dsa, klo[:, sl])
        dk = nn(qthi, dsa)
        dv = nn(gthi, pa)
        if c == 0:
            dk = jnp.concatenate([dk[:, :span] + dk3, dk[:, span:]], 1)
            dv = jnp.concatenate([dv[:, :span] + dv3, dv[:, span:]], 1)
        put(dk, hl, dl_ref, dhl, ddl_ref, 0, 0, sl)
        put(dv, hl, dl_ref, dhl, ddl_ref, 4, 128, sl)
    for c in range(0, nk, chunk):
        sl = slice(c, c + chunk)
        on = cond[:, sl] > 0.5
        s = nn(qboth, ksel[:, sl]) + bs_ref[0][:, sl]
        if c == 0:
            s = jnp.concatenate([s[:, :span] + tri, s[:, span:]], 1)
        pb = jnp.exp(s - jnp.where(on, lselo, lsehi))
        dpb = nn(gboth, vsel[:, sl])
        dsb = (pb * (dpb - jnp.where(on, dello, delhi))).astype(BF16)
        pb = pb.astype(BF16)
        dq2 = dq2 + nt(dsb, ksel[:, sl])
        dk = nn(qtboth, dsb)
        dv = nn(gtboth, pb)
        dk = jnp.where(on, dk[:128], dk[128:])
        dv = jnp.where(on, dv[:128], dv[128:])
        put(dk, hs, ds_ref, dhs, dds_ref, 0, 0, sl)
        put(dv, hs, ds_ref, dhs, dds_ref, 4, 128, sl)
    dqlo = unstack_heads(dq2[:, :128] + dq3)
    dqhi = unstack_heads(dq2[:, 128:] + dq1)
    dqt = (jnp.concatenate([dqlo, dqhi], 0) * (0.125 / 6.0)).T
    for r in range(6):
        total = None
        for h in range(2):
            part = dqt[64 * h:64 * h + 64]
            j = 2 * r + h
            dqh_ref[0, 0, j:j + 1, :] = jnp.sum(part * qr[64 * r:64 * r + 64], 0, keepdims=True)
            term = part * qh[j:j + 1]
            total = term if total is None else total + term
        dqr_ref[0, 64 * r:64 * r + 64, :] += total

def attend_back(qh, qr, hl, hs, dl, ds, cond, bl, bs, lse, o, g):
    rows, pairs, _, nq = qh.shape
    nk = dl.shape[-1]
    span = nq // 2
    chunk = min(512, nk)
    full = lambda *s: pl.BlockSpec((1, *s), lambda b, p: (b, *([0] * len(s))))
    pairb = lambda *s: pl.BlockSpec((1, 1, *s), lambda b, p: (b, p, *([0] * len(s))))
    tok = pl.BlockSpec((1, nq, 128), lambda b, p: (b, 0, p))
    sd = jax.ShapeDtypeStruct
    return pl.pallas_call(
        functools.partial(attend_back_kernel, span, chunk),
        grid=(rows, pairs),
        out_shape=[sd((rows, pairs, 12, nq), F32), sd((rows, 384, nq), F32), sd((rows, pairs, 8, nk), F32), sd((rows, pairs, 8, nk), F32),
                   sd((rows, 256, nk), F32), sd((rows, 256, nk), F32)],
        in_specs=[pairb(12, nq), full(384, nq), pairb(8, nk), pairb(8, nk), full(256, nk), full(256, nk),
                  pl.BlockSpec((1, nk), lambda b, p: (0, 0)), full(1, nk), full(1, nk), full(nq, 128), tok, tok],
        out_specs=[pairb(12, nq), full(384, nq), pairb(8, nk), pairb(8, nk), full(256, nk), full(256, nk)],
        compiler_params=pltpu.CompilerParams(vmem_limit_bytes=56 << 20),
        name="attend_back",
    )(qh, qr, hl, hs, dl, ds, cond, bl, bs, lse, o, g)

class Rows:
    def __init__(self, me, pack, out, RX, RZ, xs, xr, zs, zr):
        self.me, self.pack, self.out, self.RX, self.RZ = me, pack, out, RX, RZ
        self.xs, self.xr, self.zs, self.zr = xs, xr, zs, zr

    def remote(self, src, dst, ss, rs, dev):
        return pltpu.make_async_remote_copy(src_ref=src, dst_ref=dst, send_sem=ss, recv_sem=rs, device_id=dev, device_id_type=MESH)

    def x_copy(self, b, zz):
        return self.remote(self.pack.at[b, 2 * zz + 1 - self.me.x], self.RX.at[b, zz], self.xs.at[b, zz], self.xr.at[b, zz], self.me.xp)

    def z_copy(self, b, zz):
        me = self.me
        return self.remote(self.mine(b, zz), self.RZ.at[b, Reduce.slot(me.z, zz)], self.zs.at[b, zz], self.zr.at[b, me.z], (2 * zz + me.x, me.batch))

    def z_recv(self, b, zz):
        me = self.me
        v = self.RZ.at[b, Reduce.slot(zz, me.z)]
        return self.remote(v, v, self.zs.at[b, zz], self.zr.at[b, zz], (2 * zz + me.x, me.batch))

    def mine(self, b, zz):
        return self.pack.at[b, 2 * zz + self.me.x]

    @staticmethod
    def add(dst, src):
        dst[...] = dst[...] + src[...]

    def begin(self, b):
        def body(i, c):
            self.x_copy(b, lax.rem(self.me.z + 1 + i, NZ)).start()
            return c
        lax.fori_loop(0, NZ, body, 0)

    def x(self, b):
        me = self.me
        def body(i, c):
            zz = lax.rem(me.z + 1 + i, NZ)
            self.x_copy(b, zz).wait_recv()
            self.add(self.mine(b, zz), self.RX.at[b, zz])
            pl.when(zz != me.z)(lambda: self.z_copy(b, zz).start())
            return c
        lax.fori_loop(0, NZ, body, 0)

    def own(self, b):
        me = self.me
        def body(i, c):
            zz = lax.rem(me.z + i, NZ)
            self.z_recv(b, zz).wait_recv()
            self.add(self.mine(b, me.z), self.RZ.at[b, Reduce.slot(zz, me.z)])
            return c
        lax.fori_loop(1, NZ, body, 0)
        self.out[b] = self.pack[b, me.seq]

    def end(self, b):
        me = self.me
        def sent(zz, c):
            self.x_copy(b, zz).wait_send()
            pl.when(zz != me.z)(lambda: self.z_copy(b, zz).wait_send())
            return c
        lax.fori_loop(0, NZ, sent, 0)

def lay_out(me, block, n, span, cond_ref, dl, ds, hl, hs):
    for i in range(n):
        j = lax.rem(me.seq + i, n)
        sl = slice(i * span, (i + 1) * span)
        on = cond_ref[:, sl] > 0.5
        low = block(j)[:256, :span].astype(F32)
        high = block(j)[:256, span:].astype(F32)
        dl[0, :, sl] = low.astype(BF16)
        ds[0, :, sl] = jnp.where(on, low, high).astype(BF16)
        low = block(j)[256:, :span].astype(F32)
        high = block(j)[256:, span:].astype(F32)
        hl[:, :, sl] = low.reshape(PAIRS, 8, span)
        hs[:, :, sl] = jnp.where(on, low, high).reshape(PAIRS, 8, span)

def pack_up(me, b, span, cond_ref, pack, ddl, dds, dhl, dhs):
    n = pack.shape[1]
    for i in range(n):
        j = lax.rem(me.seq + i, n)
        sl = slice(i * span, (i + 1) * span)
        on = cond_ref[:, sl] > 0.5
        for at, lo, se in ((0, ddl[0, :, sl], dds[0, :, sl]), (256, dhl[:, :, sl].reshape(64, span), dhs[:, :, sl].reshape(64, span))):
            rows = slice(at, at + lo.shape[0])
            pack[b, j, rows, :span] = (lo + jnp.where(on, se, 0.0)).astype(BF16)
            pack[b, j, rows, span:] = jnp.where(on, 0.0, se).astype(BF16)

FFC = 256

class Feed:
    def __init__(self, hbm, outs, grads, buf):
        self.tok, self.heads_hbm, self.cot, self.w_out, self.w_gate, self.w_up, self.w_down, self.gain = hbm
        self.output, self.d_resid, self.gain_grad = outs
        self.g_out, self.g_gate, self.g_up, self.g_down = grads
        (self.xb, self.hb, self.gb, self.n2, self.n2t, self.resid, self.acc, self.dlo, self.dhi, self.wa, self.wd, self.sg, self.su, self.sd, self.dg, self.du, self.hidt,
         self.lsem, self.wsem, self.ssem) = buf
        self.rows, self.nq, self.width = self.tok.shape
        self.count = self.rows * self.nq

    def load(self):
        out = []
        for i, (src, dst) in enumerate(((self.tok, self.xb), (self.heads_hbm, self.hb), (self.cot, self.gb))):
            for r in range(self.rows):
                out.append(pltpu.make_async_copy(src.at[r], dst.at[pl.ds(r * self.nq, self.nq)], self.lsem.at[i, r]))
        return out

    def out_part(self, j):
        return pltpu.make_async_copy(self.w_out.at[:, pl.ds(j * FFC, FFC)], self.wa.at[j], self.wsem.at[0, j])

    def weights(self, c):
        k = lax.rem(c, 2)
        at = pl.ds(pl.multiple_of(c * FFC, FFC), FFC)
        return (pltpu.make_async_copy(self.w_gate.at[:, at], self.wa.at[k], self.wsem.at[1, k]),
                pltpu.make_async_copy(self.w_up.at[:, at], self.wa.at[2 + k], self.wsem.at[1, 2 + k]),
                pltpu.make_async_copy(self.w_down.at[at], self.wd.at[k], self.wsem.at[2, k]))

    def stores(self, c):
        at = pl.ds(pl.multiple_of(c * FFC, FFC), FFC)
        return (pltpu.make_async_copy(self.sg, self.g_gate.at[:, :, at], self.ssem.at[0]),
                pltpu.make_async_copy(self.su, self.g_up.at[:, :, at], self.ssem.at[1]),
                pltpu.make_async_copy(self.sd, self.g_down.at[at], self.ssem.at[2]))

    def out_store(self, j):
        return pltpu.make_async_copy((self.sg, self.su)[j % 2], self.g_out.at[:, :, pl.ds(j * FFC, FFC)], self.ssem.at[j % 2])

    def before(self):
        parts = self.width // FFC
        loads = self.load() + [self.out_part(j) for j in range(parts)]
        for cp in loads:
            cp.start()
        for cp in loads:
            cp.wait()
        for j in range(parts):
            sl = slice(j * FFC, (j + 1) * FFC)
            self.resid[:, sl] = self.xb[:, sl].astype(F32) + nn(self.hb[...], self.wa[j])
        for cp in self.weights(0):
            cp.start()
        gain = self.gain[...]
        for r in range(0, self.count, 128):
            sl = slice(r, r + 128)
            v = self.resid[sl, :]
            self.acc[sl, :] = v
            n2 = v * lax.rsqrt(jnp.mean(v * v, -1, keepdims=True) + 1e-6) * gain
            self.n2[sl, :] = n2.astype(BF16)
            self.n2t[:, sl] = n2.T.astype(BF16)
        self.dlo[...] = jnp.zeros_like(self.dlo)
        self.dhi[...] = jnp.zeros_like(self.dhi)

    def block(self, c, total):
        k = lax.rem(c, 2)
        for cp in self.weights(c):
            cp.wait()
        @pl.when(c + 1 < total)
        def _():
            for cp in self.weights(c + 1):
                cp.start()
        half = self.count // 2
        for r, dn in ((0, self.dlo), (half, self.dhi)):
            sl = slice(r, r + half)
            gate = nn(self.n2[sl, :], self.wa[k])
            up = nn(self.n2[sl, :], self.wa[2 + k])
            dh = nt(self.gb[sl, :], self.wd[k])
            sigma = 1.0 / (1.0 + jnp.exp(-gate))
            silu = gate * sigma
            hid = (silu * up).astype(BF16)
            d_gate = (dh * up * sigma * (1.0 + gate * (1.0 - sigma))).astype(BF16)
            d_up = (dh * silu).astype(BF16)
            self.dg[sl, :] = d_gate
            self.du[sl, :] = d_up
            self.hidt[:, sl] = hid.astype(F32).T.astype(BF16)
            self.acc[sl, :] += nn(hid, self.wd[k])
            dn[0] += nt(d_gate, self.wa[k]) + nt(d_up, self.wa[2 + k])
        @pl.when(c >= 1)
        def _():
            for cp in self.stores(c - 1):
                cp.wait()
        self.sg[...] = nn(self.n2t[...], self.dg[...]).astype(BF16).reshape(self.sg.shape)
        self.su[...] = nn(self.n2t[...], self.du[...]).astype(BF16).reshape(self.su.shape)
        self.sd[...] = nn(self.hidt[...], self.gb[...]).astype(BF16)
        for cp in self.stores(c):
            cp.start()

    def settle(self, c):
        for cp in self.stores(c):
            cp.wait()

    def after(self, total):
        parts = self.width // FFC
        for j in range(parts):
            self.out_part(j).start()
        gain = self.gain[...]
        sums = jnp.zeros((8, self.width), F32)
        half = self.count // 2
        for r in range(0, self.count, 128):
            sl = slice(r, r + 128)
            dn = self.dlo[0, r:r + 128] if r < half else self.dhi[0, r - half:r - half + 128]
            v = self.resid[sl, :]
            scale = lax.rsqrt(jnp.mean(v * v, -1, keepdims=True) + 1e-6)
            unit = v * scale
            prod = dn * unit
            sums = sums + jnp.sum(prod.reshape(16, 8, self.width), 0)
            e2 = dn * gain
            d = self.gb[sl, :].astype(F32) + scale * (e2 - unit * jnp.mean(e2 * unit, -1, keepdims=True))
            self.resid[sl, :] = d
            self.gb[sl, :] = d.astype(BF16)
            self.xb[sl, :] = self.acc[sl, :].astype(BF16)
            self.n2t[:, sl] = self.hb[sl, :].astype(F32).T.astype(BF16)
        self.gain_grad[...] = jnp.sum(sums, 0, keepdims=True)
        for cp in self.results():
            cp.start()
        for j in range(parts):
            self.out_part(j).wait()
        for j in range(parts):
            if j >= 2:
                self.out_store(j - 2).wait()
            (self.sg, self.su)[j % 2][...] = nn(self.n2t[...], self.gb[:, j * FFC:(j + 1) * FFC]).astype(BF16).reshape(self.sg.shape)
            self.out_store(j).start()
        for r in range(0, self.count, 128):
            total = None
            for j in range(parts):
                part = nt(self.gb[r:r + 128, j * FFC:(j + 1) * FFC], self.wa[j])
                total = part if total is None else total + part
            self.n2[r:r + 128, :] = total.astype(BF16)
        for j in range(parts - 2, parts):
            self.out_store(j).wait()

    def results(self):
        out = []
        for r in range(self.rows):
            at = pl.ds(r * self.nq, self.nq)
            out.append(pltpu.make_async_copy(self.xb.at[at], self.output.at[r], self.lsem.at[0, r]))
            out.append(pltpu.make_async_copy(self.resid.at[at], self.d_resid.at[r], self.lsem.at[1, r]))
        return out

def back_kernel(span, chunk, units, plan, blocks, qh_ref, qr_ref, shared_ref, cond_ref, bl_ref, bs_ref, lse_ref, *refs):
    feed_in, refs = refs[:8], refs[8:]
    dqh_ref, dqr_ref, mine_ref, output, d_resid, gain_grad = refs[:6]
    sums, grads, refs = refs[6:10], refs[10:14], refs[14:]
    dl, ds, hl, hs, ddl, dds, dhl, dhs, pack, RX, RZ, xs, xr, zs, zr, bsem = refs[:16]
    fb, refs = refs[16:34], refs[34:]
    me = Place()
    b, p = pl.program_id(0), pl.program_id(1)
    step = b * PAIRS + p
    nq = 2 * span
    red = Reduce(me, units, grads, sums, refs)
    row = Rows(me, pack, mine_ref, RX, RZ, xs, xr, zs, zr)
    feed = Feed(feed_in, (output, d_resid, gain_grad), grads, (*fb[:7], ddl, dds, *fb[7:]))

    def act(items):
        for it in items:
            if it[0] == "row":
                getattr(row, it[1])(it[2])
            elif it[0] == "settle":
                feed.settle(it[1])
            elif it[0] == "results":
                for cp in feed.results():
                    cp.wait()
            else:
                red.run([it])

    brought = [pltpu.make_async_copy(shared_ref.at[:, r], pack.at[r], bsem.at[r]) for r in range(pack.shape[0])]

    @pl.when(step == 0)
    def _():
        greet(me)
        for cp in brought:
            cp.start()
        feed.before()
        def body(c, carry):
            feed.block(c, blocks)
            for k, items in plan["feed"].items():
                pl.when(c == k)(functools.partial(act, items))
            return carry
        lax.fori_loop(0, blocks, body, 0)
        feed.settle(blocks - 1)
        act(plan["mid"])
        feed.after(blocks)
        act(plan["first"])
        for cp in brought:
            cp.wait()

    @pl.when(p == 0)
    def _():
        lay_out(me, lambda j: pack.at[b, j], 2 * NZ, span, cond_ref, dl, ds, hl, hs)
        dqr_ref[...] = jnp.zeros_like(dqr_ref)
        ddl[...] = jnp.zeros_like(ddl)
        dds[...] = jnp.zeros_like(dds)

    rows_at = pl.ds(pl.multiple_of(b * nq, nq), nq)
    lanes_at = pl.ds(pl.multiple_of(p * 128, 128), 128)
    pair_back(span, chunk, p, qh_ref, qr_ref, Pair(hl, p), Pair(hs, p), dl, ds, cond_ref, bl_ref, bs_ref, lse_ref,
              feed.hb[rows_at, lanes_at], feed.n2[rows_at, lanes_at], dqh_ref, dqr_ref, Pair(dhl, p), Pair(dhs, p), ddl, dds)

    @pl.when(p == PAIRS - 1)
    def _():
        pack_up(me, b, span, cond_ref, pack, ddl, dds, dhl, dhs)
        row.begin(b)

    for s, items in plan["steps"].items():
        pl.when(step == s)(functools.partial(act, items))

def backward(qh, qr, shared, cond, bl, bs, lse, tokens, heads_out, cotangent, w_out, w_gate, w_up, w_down, gain_two, units, plan, cid):
    rows, pairs, _, nq = qh.shape
    n = shared.shape[0]
    span = nq // 2
    nk = n * span
    width, ff = w_gate.shape
    count = rows * nq
    full = lambda *s: pl.BlockSpec((1, *s), lambda b, p: (b, *([0] * len(s))))
    pairb = lambda *s: pl.BlockSpec((1, 1, *s), lambda b, p: (b, p, *([0] * len(s))))
    sd = jax.ShapeDtypeStruct
    DMA = pltpu.SemaphoreType.DMA
    V = pltpu.VMEM
    whole = pl.BlockSpec(memory_space=pltpu.VMEM)
    far = pl.BlockSpec(memory_space=pl.ANY)
    part = shared.shape[2:]
    scratch = [V((1, 256, nk), BF16)] * 2 + [V((PAIRS, 8, nk), F32)] * 2 + [V((1, 256, nk), F32)] * 2 + [V((PAIRS, 8, nk), F32)] * 2
    scratch += [V((rows, n, *part), BF16), V((rows, NZ, *part), BF16), V((rows, NZ - 1, *part), BF16)] + [DMA((rows, NZ))] * 4 + [DMA((rows,))]
    scratch += [V((count, width), BF16)] * 4 + [V((width, count), BF16)] + [V((count, width), F32)] * 2
    scratch += [V((4, width, FFC), BF16), V((2, FFC, width), BF16)] + [V((n, width // n, FFC), BF16)] * 2 + [V((FFC, width), BF16)] + [V((count, FFC), BF16)] * 2 + [V((FFC, count), BF16)]
    scratch += [DMA((3, rows)), DMA((3, 4)), DMA((3,))]
    shard = (n, width // n)
    sums = [sd((width // n, width), BF16), sd((width // n, ff), BF16), sd((width // n, ff), BF16), sd((ff // n, width), BF16)]
    grads = [sd((*shard, width), BF16), sd((*shard, ff), BF16), sd((*shard, ff), BF16), sd((ff, width), BF16)]
    return pl.pallas_call(
        functools.partial(back_kernel, span, min(512, nk), units, plan, ff // FFC),
        grid=(rows, pairs),
        out_shape=[sd((rows, pairs, 12, nq), F32), sd((rows, 384, nq), F32), sd((rows, *part), BF16), sd((rows, nq, width), BF16),
                   sd((rows, nq, width), F32), sd((1, width), F32)] + sums + grads,
        in_specs=[pairb(12, nq), full(384, nq), far, pl.BlockSpec((1, nk), lambda b, p: (0, 0)), full(1, nk), full(1, nk), full(nq, 128)] + [far] * 7 + [whole],
        out_specs=[pairb(12, nq), full(384, nq), whole, far, far, whole] + [far] * 8,
        scratch_shapes=scratch + reduce_scratch(units),
        compiler_params=pltpu.CompilerParams(collective_id=cid, has_side_effects=True, vmem_limit_bytes=60 << 20),
        name="backward",
    )(qh, qr, shared, cond, bl, bs, lse, tokens, heads_out, cotangent, w_out, w_gate, w_up, w_down, gain_two)[:10]

class Gather:
    def __init__(self, me, units, ins, outs, sems):
        self.me, self.units, self.ins, self.outs = me, units, ins, outs
        self.zs, self.zr, self.xs, self.xr, self.ys, self.yr, self.cs, self.cr, self.ls = sems

    def remote(self, src, dst, ss, rs, dev):
        return pltpu.make_async_remote_copy(src_ref=src, dst_ref=dst, send_sem=ss, recv_sem=rs, device_id=dev, device_id_type=MESH)

    def view(self, k, shard, y, c):
        u = self.units[k]
        return self.part(u, self.outs[u.arr].at[shard], y, c)

    @staticmethod
    def part(u, ref, y, c):
        return rect(u, ref, 2 * c + y, 4) if u.flow == "P" else rect(u, ref, c, 2)

    def first(self, k, ss, rs, dev):
        u, me = self.units[k], self.me
        return self.remote(self.part(u, self.ins[u.arr], me.y, me.c), self.view(k, me.seq, me.y, me.c), ss, rs, dev)

    def onward(self, k, shard, y, ss, rs, dev):
        v = self.view(k, shard, y, self.me.c)
        return self.remote(v, v, ss, rs, dev)

    def zsend(self, k, zz):
        return self.first(k, self.zs.at[k, zz], self.zr.at[k, self.me.z], (2 * zz + self.me.x, self.me.batch))

    def zrecv(self, k, zz):
        me = self.me
        return self.onward(k, 2 * zz + me.x, me.y, self.zs.at[k, zz], self.zr.at[k, zz], (2 * zz + me.x, me.batch))

    def xown(self, k):
        return self.first(k, self.xs.at[k, self.me.z], self.xr.at[k, self.me.z], self.me.xp)

    def xsend(self, k, zz):
        return self.onward(k, 2 * zz + self.me.x, self.me.y, self.xs.at[k, zz], self.xr.at[k, zz], self.me.xp)

    def xrecv(self, k, zz):
        return self.onward(k, 2 * zz + 1 - self.me.x, self.me.y, self.xs.at[k, zz], self.xr.at[k, zz], self.me.xp)

    def ycopy(self, k, shard, mine):
        return self.onward(k, shard, self.me.y if mine else 1 - self.me.y, self.ys.at[k, shard], self.yr.at[k, shard], self.me.yp)

    def ccopy(self, k, w, shard):
        return self.onward(k, shard, self.me.y if w == 0 else 1 - self.me.y, self.cs.at[k, w, shard], self.cr.at[k, w, shard], self.me.cp)

    def crecv(self, k, w, shard):
        v = self.view(k, shard, self.me.y if w == 0 else 1 - self.me.y, 1 - self.me.c)
        return self.remote(v, v, self.cs.at[k, w, shard], self.cr.at[k, w, shard], self.me.cp)

    def local(self, a):
        return pltpu.make_async_copy(self.ins[a], self.outs[a].at[self.me.seq], self.ls.at[a])

    def other(self, i):
        return lax.rem(self.me.z + i, NZ)

    def begin(self, k, i):
        self.zsend(k, self.other(i)).start()
        pl.when(i == 1)(lambda: self.xown(k).start())

    def spread(self, k, shard):
        if self.units[k].flow == "P":
            self.ycopy(k, shard, True).start()
        self.ccopy(k, 0, shard).start()

    def z(self, k, i):
        zz = self.other(i)
        self.zrecv(k, zz).wait_recv()
        self.xsend(k, zz).start()
        self.spread(k, 2 * zz + self.me.x)

    def x(self, k, i):
        zz = self.other(i)
        self.xrecv(k, zz).wait_recv()
        self.spread(k, 2 * zz + 1 - self.me.x)

    def far(self, i):
        return 2 * self.other(i) + jnp.where(i < NZ, self.me.x, 1 - self.me.x)

    def y(self, k, i):
        shard = self.far(i)
        self.ycopy(k, shard, False).wait_recv()
        self.ccopy(k, 1, shard).start()

    def got(self, k, i):
        for w in range(2 if self.units[k].flow == "P" else 1):
            self.crecv(k, w, self.far(i)).wait_recv()

    def sent(self, k, i):
        me = self.me
        pl.when(i < NZ)(lambda: self.zsend(k, self.other(i)).wait_send())
        pl.when(i < NZ)(lambda: self.xsend(k, self.other(i)).wait_send())
        pl.when(i == NZ)(lambda: self.xown(k).wait_send())
        shard = self.far(i)
        self.ccopy(k, 0, shard).wait_send()
        if self.units[k].flow == "P":
            self.ycopy(k, shard, True).wait_send()
            self.ccopy(k, 1, shard).wait_send()

    def run(self, plan):
        for step, k, first, n in plan:
            fn = getattr(self, step)
            def body(i, c):
                fn(k, i)
                return c
            lax.fori_loop(first, first + n, body, 0)

class RowsGather:
    def __init__(self, me, shared, zs, zr, xs, xr):
        self.me, self.shared, self.zs, self.zr, self.xs, self.xr = me, shared, zs, zr, xs, xr

    def copy(self, b, shard, ss, rs, dev):
        v = self.shared.at[shard, b]
        return pltpu.make_async_remote_copy(src_ref=v, dst_ref=v, send_sem=ss, recv_sem=rs, device_id=dev, device_id_type=MESH)

    def zsend(self, b, zz):
        me = self.me
        return self.copy(b, me.seq, self.zs.at[b, zz], self.zr.at[b, me.z], (2 * zz + me.x, me.batch))

    def zrecv(self, b, zz):
        me = self.me
        return self.copy(b, 2 * zz + me.x, self.zs.at[b, zz], self.zr.at[b, zz], (2 * zz + me.x, me.batch))

    def xsend(self, b, zz):
        return self.copy(b, 2 * zz + self.me.x, self.xs.at[b, zz], self.xr.at[b, zz], self.me.xp)

    def xrecv(self, b, zz):
        return self.copy(b, 2 * zz + 1 - self.me.x, self.xs.at[b, zz], self.xr.at[b, zz], self.me.xp)

    def loop(self, first, fn):
        def body(i, c):
            fn(lax.rem(self.me.z + i, NZ))
            return c
        lax.fori_loop(first, NZ, body, 0)

    def begin(self, b):
        self.loop(1, lambda zz: self.zsend(b, zz).start())
        self.xsend(b, self.me.z).start()

    def z(self, b):
        def one(zz):
            self.zrecv(b, zz).wait_recv()
            self.xsend(b, zz).start()
        self.loop(1, one)

    def x(self, b):
        self.loop(0, lambda zz: self.xrecv(b, zz).wait_recv())

    def end(self, b):
        self.loop(1, lambda zz: self.zsend(b, zz).wait_send())
        self.loop(0, lambda zz: self.xsend(b, zz).wait_send())

def turn_rows(u, cosine, sine):
    out = []
    for r in range(0, u.shape[0], 64):
        a, b = u[r:r + 32], u[r + 32:r + 64]
        out += [a * cosine - b * sine, b * cosine + a * sine]
    return jnp.concatenate(out, 0)

def project(me, span, tok_ref, small_ref, cos_ref, sin_ref, normed_ref, qh_ref, qr_ref, shared_ref, b):
    nq = 2 * span
    d = tok_ref.shape[-1]
    gains = small_ref[:, :, 768:896].reshape(d, 128).astype(F32).T
    x = tok_ref[b].astype(F32)
    unit = x * lax.rsqrt(jnp.mean(x * x, -1, keepdims=True) + 1e-6)
    normed = (unit * gains[32:33]).astype(BF16)
    normed_ref[b] = normed
    w = small_ref[...].reshape(d, 896)
    f = nn(normed, w).T
    qh_ref[b] = f[:96].reshape(PAIRS, 12, nq)
    cosine, sine = cos_ref[...], sin_ref[...]
    qr_ref[b] = turn_rows(f[96:480], cosine, sine)
    own = jnp.concatenate([turn_rows(f[480:608], cosine, sine), f[608:800]], 0)
    shared_ref[me.seq, b] = own.astype(BF16)

def forward_kernel(span, chunk, units, narr, plan, tok_ref, cos_ref, sin_ref, cond_ref, bl_ref, bs_ref, *refs):
    ins = refs[:narr]
    normed_ref, qh_ref, qr_ref, shared_out, o_ref, lse_ref = refs[narr:narr + 6]
    outs = refs[narr + 6:2 * narr + 6]
    shared_ref, small, saved, dl, ds, hl, hs, s1, s2, rzs, rzr, rxs, rxr = refs[2 * narr + 6:2 * narr + 19]
    small_out, outs = outs[0], (small, *outs[1:])
    me = Place()
    b, p = pl.program_id(0), pl.program_id(1)
    step = b * PAIRS + p
    gat = Gather(me, units, ins, outs, refs[2 * narr + 19:])
    saves = (pltpu.make_async_copy(small, small_out, saved.at[0]), pltpu.make_async_copy(shared_ref, shared_out, saved.at[1]))
    row = RowsGather(me, shared_ref, rzs, rzr, rxs, rxr)

    def act(items):
        for it in items:
            if it[0] == "row":
                getattr(row, it[1])(it[2])
            elif it[0] == "project":
                for r in range(tok_ref.shape[0]):
                    project(me, span, tok_ref, small, cos_ref, sin_ref, normed_ref, qh_ref, qr_ref, shared_ref, r)
            elif it[0] == "local":
                for a in range(narr):
                    gat.local(a).start()
                gat.local(0).wait()
            elif it[0] == "locals":
                for a in range(1, narr):
                    gat.local(a).wait()
                for save in saves:
                    save.start()
                for save in saves:
                    save.wait()
            else:
                gat.run([it])

    @pl.when(step == 0)
    def _():
        greet(me)
        act(plan["first"])

    @pl.when(p == 0)
    def _():
        lay_out(me, lambda j: shared_ref.at[j, b], 2 * NZ, span, cond_ref, dl, ds, hl, hs)

    pair_forward(span, chunk, p, qh_ref[b, p], qr_ref[b], hl[p], hs[p], dl, ds, cond_ref, bl_ref, bs_ref, o_ref, lse_ref, s1, s2)

    for s, items in plan["steps"].items():
        pl.when(step == s)(functools.partial(act, items))

def forward(tokens, cosine, sine, cond, bl, bs, weights, units, plan, cid):
    rows, nq, width = tokens.shape
    span = nq // 2
    n = 2 * NZ
    nk = n * span
    narr, nu = len(weights), len(units)
    chunk = min(512, nk)
    whole = pl.BlockSpec(memory_space=pltpu.VMEM)
    far = pl.BlockSpec(memory_space=pl.ANY)
    full = lambda *s: pl.BlockSpec((1, *s), lambda b, p: (b, *([0] * len(s))))
    sd = jax.ShapeDtypeStruct
    DMA = pltpu.SemaphoreType.DMA
    V = pltpu.VMEM
    scratch = [V((n, rows, 320, nq), BF16), V((n, *weights[0].shape), BF16), DMA((2,))] + [V((1, 256, nk), BF16)] * 2 + [V((PAIRS, 8, nk), F32)] * 2 + [V((nq, nk), F32)] * 2 + [DMA((rows, NZ))] * 4
    scratch += [DMA((nu, NZ))] * 4 + [DMA((nu, n))] * 2 + [DMA((nu, 2, n))] * 2 + [DMA((narr,))]
    return pl.pallas_call(
        functools.partial(forward_kernel, span, chunk, units, narr, plan),
        grid=(rows, PAIRS),
        out_shape=[sd((rows, nq, width), BF16), sd((rows, PAIRS, 12, nq), F32), sd((rows, 384, nq), F32), sd((n, rows, 320, nq), BF16),
                   sd((rows, nq, width), BF16), sd((rows, nq, 128), F32)] + [sd((n, *a.shape), a.dtype) for a in weights],
        in_specs=[whole, whole, whole, pl.BlockSpec((1, nk), lambda b, p: (0, 0)), full(1, nk), full(1, nk)] + [far] * narr,
        out_specs=[whole, whole, whole, far, pl.BlockSpec((1, nq, 128), lambda b, p: (b, 0, p)), full(nq, 128)] + [far] * narr,
        scratch_shapes=scratch,
        compiler_params=pltpu.CompilerParams(collective_id=cid, has_side_effects=True, vmem_limit_bytes=56 << 20),
        name="forward",
    )(tokens, cosine, sine, cond, bl, bs, *weights)

HEADS, HDIM, QRANK, KVRANK = 16, 64, 6, 2
PAIRS = HEADS // 2
EPSILON = 1e-06


def rms_forward(values, gain):
    scale = lax.rsqrt(jnp.mean(values * values, -1, keepdims=True) + EPSILON)
    unit = values * scale
    return (unit * gain, unit, scale)


def rms_backward(grad_out, unit, scale, gain):
    scaled = grad_out * gain
    grad_in = scale * (scaled - unit * jnp.mean(scaled * unit, -1, keepdims=True))
    return (grad_in, jnp.sum(grad_out * unit, 0))


def rotation(positions):
    half = HDIM // 2
    index = jnp.arange(half).astype(F32)
    inverse = jnp.exp(index * (-math.log(10000.0) / half))
    angles = inverse[:, None] * positions.astype(F32)[None, :]
    return (jnp.cos(angles), jnp.sin(angles))


def rotate(u, cosine, sine):
    rows, depth, slots = u.shape
    v = u.reshape(rows, depth // HDIM, HDIM, slots)
    a, b = v[:, :, :HDIM // 2], v[:, :, HDIM // 2:]
    return jnp.concatenate([a * cosine - b * sine, b * cosine + a * sine], 2).reshape(u.shape)


def dot(a, b, ca, cb):
    return lax.dot_general(a, b, ((ca, cb), ((), ())), preferred_element_type=F32)


def pair_columns(a, ranks):
    return a.reshape(-1, ranks, PAIRS, 2).transpose(0, 2, 1, 3).reshape(a.shape)


def head_columns(a, ranks):
    return a.reshape(-1, PAIRS, ranks, 2).transpose(0, 2, 1, 3).reshape(a.shape)


GATHER_UNITS = [
    Unit(0, (0, 128), (0, 896), "P", 0), Unit(1, (0, 128), (0, 1024), "P", 0),
    Unit(2, (0, 128), (0, 1408), "P", 0), Unit(2, (0, 128), (1408, 1408), "P", 0),
    Unit(3, (0, 128), (0, 1408), "R", 0), Unit(3, (0, 128), (1408, 1408), "P", 0),
    Unit(4, (0, 176), (0, 1024), "P", 1), Unit(4, (176, 176), (0, 1024), "P", 1)]
GATHER_PLAN = {
    "first": [("local",), ("begin", 0, 1, 3), ("begin", 1, 1, 3), ("z", 0, 1, 3), ("x", 0, 0, 4), ("begin", 3, 1, 3), ("y", 0, 1, 7), ("begin", 7, 1, 3), ("begin", 2, 1, 3), ("z", 1, 1, 3), ("got", 0, 1, 7), ("x", 1, 0, 4), ("begin", 6, 1, 3), ("z", 3, 1, 3), ("project",), ("z", 2, 1, 3), ("x", 3, 0, 4), ("row", "begin", 0), ("row", "begin", 1), ("x", 2, 0, 4), ("z", 7, 1, 3), ("row", "z", 0), ("z", 6, 1, 3), ("row", "x", 0), ("y", 3, 4, 4), ("y", 2, 1, 3), ("begin", 5, 1, 3), ("begin", 4, 1, 3), ("y", 7, 1, 3)],
    "steps": {
        2: [("x", 6, 0, 4), ("y", 1, 1, 3), ("y", 3, 1, 3), ("row", "z", 1)],
        5: [("z", 5, 1, 3), ("y", 1, 4, 4)],
        6: [("x", 7, 0, 4)],
        7: [("y", 2, 4, 4), ("row", "x", 1)],
        10: [("z", 4, 1, 3), ("x", 5, 0, 4)],
        12: [("y", 7, 4, 4), ("y", 6, 1, 3)],
        13: [("y", 6, 4, 4), ("y", 5, 1, 3)],
        14: [("x", 4, 0, 4)],
        15: [("y", 5, 4, 4), ("got", 1, 1, 7), ("got", 2, 1, 7), ("got", 3, 1, 7), ("got", 4, 1, 7), ("got", 5, 1, 7), ("got", 6, 1, 7), ("got", 7, 1, 7), ("locals",), ("sent", 0, 1, 7), ("sent", 1, 1, 7), ("sent", 2, 1, 7), ("sent", 3, 1, 7), ("sent", 4, 1, 7), ("sent", 5, 1, 7), ("sent", 6, 1, 7), ("sent", 7, 1, 7), ("row", "end", 0), ("row", "end", 1)],
    },
}
REDUCE_UNITS = [
    Unit(1, (0, 128), (0, 1024), "P", 0), Unit(2, (0, 128), (0, 1024), "R", 0),
    Unit(1, (0, 128), (1024, 1024), "P", 0), Unit(2, (0, 128), (1024, 1024), "R", 0),
    Unit(1, (0, 128), (2048, 768), "P", 0), Unit(2, (0, 128), (2048, 768), "P", 0),
    Unit(3, (0, 176), (0, 1024), "P", 1), Unit(3, (176, 176), (0, 1024), "P", 1), Unit(0, (0, 128), (0, 1024), "P", 0)]
REDUCE_PLAN = {
    "feed": {
        4: [("begin", 0, 0, 8), ("begin", 1, 0, 8)],
        5: [("core", 0, 0, 4)],
        6: [("core", 1, 0, 4), ("core", 0, 4, 4)],
        7: [("y", 0, 0, 4)],
        8: [("begin", 2, 0, 8), ("begin", 3, 0, 8)],
        9: [("core", 2, 0, 4), ("y", 0, 4, 4), ("core", 1, 4, 4)],
    },
    "mid": [("begin", 5, 0, 8), ("begin", 7, 0, 8), ("x", 1, 0, 4), ("core", 2, 4, 4), ("core", 3, 0, 4), ("core", 5, 0, 4)],
    "first": [("begin", 4, 0, 8), ("core", 5, 4, 4), ("begin", 8, 0, 8), ("y", 2, 0, 4)],
    "steps": {
        0: [("y", 2, 4, 4), ("core", 4, 4, 4), ("core", 3, 4, 4), ("core", 7, 0, 4), ("x", 3, 0, 4), ("y", 5, 0, 4), ("core", 4, 0, 4)],
        2: [("core", 7, 4, 4), ("y", 5, 4, 4), ("x", 5, 0, 4)],
        4: [("y", 7, 0, 4), ("x", 0, 0, 4)],
        5: [("x", 2, 0, 4)],
        6: [("y", 4, 4, 4), ("y", 4, 0, 4), ("core", 8, 4, 4)],
        7: [("begin", 6, 0, 8), ("y", 7, 4, 4), ("x", 4, 0, 4), ("x", 7, 0, 4), ("core", 8, 0, 4)],
        8: [("core", 6, 0, 4)],
        10: [("y", 8, 0, 4), ("core", 6, 4, 4), ("row", "x", 0)],
        11: [("own", 5, 0, 1), ("own", 2, 0, 1), ("own", 7, 0, 1), ("y", 8, 4, 4), ("own", 4, 0, 1), ("y", 6, 0, 4)],
        12: [("x", 8, 0, 4)],
        13: [("y", 6, 4, 4)],
        14: [("last", 2, 0, 1), ("x", 6, 0, 4), ("last", 7, 0, 1)],
        15: [("own", 8, 0, 1), ("own", 1, 0, 1), ("row", "own", 0), ("own", 3, 0, 1), ("own", 0, 0, 1), ("row", "x", 1), ("last", 1, 0, 1), ("own", 6, 0, 1), ("last", 8, 0, 1), ("last", 0, 0, 1), ("last", 6, 0, 1), ("last", 4, 0, 1), ("last", 5, 0, 1), ("last", 3, 0, 1), ("row", "own", 1), ("end", 0, 0, 1), ("end", 1, 0, 1), ("end", 2, 0, 1), ("end", 3, 0, 1), ("end", 4, 0, 1), ("end", 5, 0, 1), ("end", 6, 0, 1), ("end", 7, 0, 1), ("end", 8, 0, 1), ("results",), ("row", "end", 0), ("row", "end", 1)],
    },
}
SMALL_UNITS = [Unit(0, (0, 128), (0, 896), "P", 0)]
SMALL_PLAN = [("begin", 0, 0, 8), ("core", 0, 0, 8), ("y", 0, 0, 8), ("x", 0, 0, 4), ("own", 0, 0, 1), ("last", 0, 0, 1), ("end", 0, 0, 1)]


def reduce_far(arrays):
    out = []
    for a in arrays:
        own = lax.psum_scatter(a.astype(F32), "seq", scatter_dimension=0, tiled=True)[0]
        out.append(lax.psum(own.astype(BF16), "batch"))
    return out


def per_device(near, tokens, cotangent, lengths, span_order, attn_gain, query_heads, query_dims, key_heads, key_dims,
               value_heads, value_dims, out_proj, ffn_gain, gate_proj, up_proj, down_proj):
    rows, slots, width = tokens.shape
    span = slots // 2
    count = rows * slots
    nseq = span_order.shape[0]
    nk = nseq * span
    me = lax.axis_index("seq")
    key_value_heads = pair_columns(jnp.concatenate([key_heads, value_heads], 1), 4)
    small = jnp.concatenate([pair_columns(query_heads, QRANK), query_dims, key_dims, value_dims, key_value_heads, attn_gain[:, None], ffn_gain[:, None]], 1)
    small = jnp.pad(small, ((0, 0), (0, 896 - small.shape[1])))
    offsets = jnp.arange(span, dtype=jnp.int32)
    spans = jnp.concatenate([span_order, span_order], 0)
    spans = lax.dynamic_slice_in_dim(spans, me, nseq, 0)
    local_pos = (spans[0][:, None] * span + offsets[None, :]).reshape(-1)
    cosine, sine = rotation(local_pos)
    chosen = spans[:, 0] < spans[0, 0]
    low_pos = (spans[:, 0][:, None] * span + offsets[None, :]).reshape(1, nk)
    sel_pos = (jnp.where(chosen, spans[:, 0], spans[:, 1])[:, None] * span + offsets[None, :]).reshape(1, nk)
    cond = jnp.repeat(chosen.astype(F32), span).reshape(1, nk)
    low_bias = jnp.where(low_pos < lengths[:, None], 0.0, NEG)[:, None, :]
    sel_bias = jnp.where(sel_pos < lengths[:, None], 0.0, NEG)[:, None, :]

    masks = (cond, low_bias, sel_bias)
    flat = tokens.reshape(count, width).astype(F32)
    weights = [small, out_proj, gate_proj, up_proj, down_proj]
    if near:
        by_row, qh, qr, shared, heads_out, lse, *parts = forward(tokens, cosine, sine, *masks, weights, GATHER_UNITS, GATHER_PLAN, 0)
    else:
        parts = [lax.all_gather(a, "seq", axis=0) for a in weights]
    small, w_out, w_gate, w_up, w_down = [p.reshape(-1, p.shape[-1]) for p in parts]
    w_qkv = small[:, :800]
    gain_one = small[:, 800].astype(F32)
    gain_two = small[:, 801].astype(F32)
    normed_full, unit_one, scale_one = rms_forward(flat, gain_one)
    if not near:
        by_row = normed_full.astype(BF16).reshape(rows, slots, width)
        factors = jnp.stack([dot(w_qkv, by_row[b], (0,), (1,)) for b in range(rows)])
        qh = factors[:, :96].reshape(rows, PAIRS, 12, slots)
        qr = rotate(factors[:, 96:480], cosine, sine)
        own = jnp.concatenate([rotate(factors[:, 480:608], cosine, sine), factors[:, 608:800]], 1).astype(BF16)
        shared = lax.all_gather(own, "seq", axis=0)
        turned = lax.dynamic_slice_in_dim(jnp.concatenate([shared, shared], 0), me, nseq, 0)
        low, high = turned[..., :span], turned[..., span:]
        sel = jnp.where(chosen[:, None, None, None], low, high)
        low = low.transpose(1, 2, 0, 3).reshape(rows, 320, nk)
        sel = sel.transpose(1, 2, 0, 3).reshape(rows, 320, nk)
        in_pairs = lambda a: a[:, 256:].astype(F32).reshape(rows, PAIRS, 8, nk)
        factors = (in_pairs(low), in_pairs(sel), low[:, :256], sel[:, :256])
        heads_out, lse = attend(qh, qr, *factors, *masks)
    if near:
        dqh, dqr, mine, output, d_resid, gain_two_grad, *sums = backward(
            qh, qr, shared, *masks, lse, tokens, heads_out, cotangent, w_out, w_gate, w_up, w_down, gain_two[None, :], REDUCE_UNITS, REDUCE_PLAN, 1)
        d_resid, gain_two_grad = d_resid.reshape(count, width), gain_two_grad[0]
    else:
        heads_flat = heads_out.reshape(count, width)

        resid = flat + dot(heads_flat, w_out, (1,), (0,))
        normed_two_full, unit_two, scale_two = rms_forward(resid, gain_two)
        normed_two = normed_two_full.astype(BF16)
        gate = dot(normed_two, w_gate, (1,), (0,))
        up_part = dot(normed_two, w_up, (1,), (0,))
        sigma = jax.nn.sigmoid(gate)
        hidden = (gate * sigma * up_part).astype(BF16)
        output = (resid + dot(hidden, w_down, (1,), (0,))).astype(BF16).reshape(rows, slots, width)

        grad_out = cotangent.reshape(count, width)
        down_grad = dot(hidden, grad_out, (0,), (0,)).astype(BF16)
        d_hidden = dot(grad_out, w_down, (1,), (1,))
        d_gate = (d_hidden * up_part * sigma * (1.0 + gate * (1.0 - sigma))).astype(BF16)
        d_up = (d_hidden * gate * sigma).astype(BF16)
        gate_grad = dot(normed_two, d_gate, (0,), (0,)).astype(BF16)
        up_grad = dot(normed_two, d_up, (0,), (0,)).astype(BF16)
        d_normed_two = dot(d_gate, w_gate, (1,), (1,)) + dot(d_up, w_up, (1,), (1,))
        d_mid, gain_two_grad = rms_backward(d_normed_two, unit_two, scale_two, gain_two)
        d_resid = grad_out.astype(F32) + d_mid
        d_attn = d_resid.astype(BF16)
        out_grad = dot(heads_flat, d_attn, (0,), (0,)).astype(BF16)
        d_heads = dot(d_attn, w_out, (1,), (1,)).astype(BF16).reshape(rows, slots, width)

        grads = [g.reshape(nseq, -1, g.shape[-1]) for g in (out_grad, gate_grad, up_grad, down_grad)]
        dqh, dqr, dhl, dhs, ddl, dds = attend_back(qh, qr, *factors, *masks, lse, heads_out, d_heads)
        from_low = jnp.concatenate([ddl, dhl.reshape(rows, 64, nk)], 1).reshape(rows, 320, nseq, span)
        from_sel = jnp.concatenate([dds, dhs.reshape(rows, 64, nk)], 1).reshape(rows, 320, nseq, span)
        pick = chosen[None, None, :, None]
        both = jnp.concatenate([from_low + jnp.where(pick, from_sel, 0.0), jnp.where(pick, 0.0, from_sel)], -1).transpose(2, 0, 1, 3)
        both = lax.dynamic_slice_in_dim(jnp.concatenate([both, both], 0), lax.rem(nseq - me, nseq), nseq, 0)
        mine = lax.psum_scatter(both, "seq", scatter_dimension=0, tiled=True)[0]
        sums = reduce_far(grads)
    mine = mine.astype(F32)
    turned = jnp.concatenate([dqh.reshape(rows, 96, slots), rotate(dqr, cosine, -sine), rotate(mine[:, :128], cosine, -sine), mine[:, 128:]], 1).astype(BF16)
    small_grad = dot(by_row, turned, (0, 1), (0, 2))
    d_normed = dot(turned, w_qkv, (1,), (1,)).reshape(count, width)
    d_first, gain_one_grad = rms_backward(d_normed, unit_one, scale_one, gain_one)
    input_grad = (d_resid + d_first).reshape(rows, slots, width)
    small_grad = jnp.concatenate([small_grad, gain_one_grad[:, None], gain_two_grad[:, None], jnp.zeros((width, 94), F32)], 1).astype(BF16)

    small_grad = small_grad.reshape(nseq, -1, 896)
    small_sum = reduce_weights([small_grad], SMALL_UNITS, SMALL_PLAN, 3)[0] if near else reduce_far([small_grad])[0]
    small_sum = small_sum.astype(F32)
    out_sum, gate_sum, up_sum, down_sum = [g.astype(F32) for g in sums]
    key_value = head_columns(small_sum[:, 736:800], 4)
    return (output, input_grad, small_sum[:, 800], head_columns(small_sum[:, :96], QRANK), small_sum[:, 96:480], key_value[:, :32], small_sum[:, 480:608],
            key_value[:, 32:], small_sum[:, 608:736], out_sum, small_sum[:, 801], gate_sum, up_sum, down_sum)


def solution(mesh):
    near = mesh.shape["seq"] == 8 and mesh.shape["batch"] == 4
    by_slot = P("batch", "seq", None)
    line, table = P("seq"), P("seq", None)
    return jax.shard_map(
        functools.partial(per_device, near),
        mesh=mesh,
        in_specs=(by_slot, by_slot, P("batch"), P(), line, *([table] * 7), line, *([table] * 3)),
        out_specs=(by_slot, by_slot, line, *([table] * 7), line, *([table] * 3)),
        check_vma=False,
    )
```

profile of v0, /device:TPU:0, one launch (start us, length us, event | category | flops | bytes accessed | tf_op | source)
XLA Modules:
  0.0 360.0 jit_solution(17768649243997976409)
XLA Ops:
  0.7 0.8 pad_add_fusion
  3.7 1.5 fusion.8
  5.9 1.3 compare_select_fusion
  8.1 0.8 copy.54
  9.0 0.8 copy.58
  9.8 0.8 copy.59
  10.6 0.8 fusion.10
  11.4 1.1 concatenate.34
  13.2 125.6 %forward.1 = (bf16[2,256,1024]{2,1,0:T(8,128)(2,1)}, f32[2,8,12,256]{3,2,1,0:T(8,128)}, f32[2,384,256]{2,1,0:T(8,128)}, bf16[8,2,320,256]{3,2,1,0:T(8,128)(2,1)}...) custom-call(bf16[2,256,1024]{2,1,0:T(8,128)(2,1)} %refs_0_.1, ...), custom_call_target="tpu_custom_call" | custom-call | tf_op jit(solution)/shard_map/forward/pallas_call | solution.py:1117
  138.9 1.2 slice_convert_fusion
  141.1 160.1 %backward.1 = (f32[2,8,12,256]{3,2,1,0:T(8,128)}, f32[2,384,256]{2,1,0:T(8,128)}, bf16[2,320,256]{2,1,0:T(8,128)(2,1)}, bf16[2,256,1024]{2,1,0:T(8,128)(2,1)}, f...) custom-call(f32[2,8,12,256]{3,2,1,0:T(8,128)} %get-tuple-element.35., ...), custom_call_target="tpu_custom_call" | custom-call | tf_op jit(solution)/shard_map/backward/pallas_call | solution.py:867
  301.2 0.8 convert_reduce_fusion
  302.0 1.0 convert.41
  303.8 1.1 slice.77
  304.9 0.9 slice.80
  306.8 1.1 concatenate.42
  307.9 2.7 fusion.7
  310.7 1.0 bitcast_convert_fusion
  312.3 1.9 fusion.6
  314.2 1.7 copy.65
  316.1 2.8 maximum_maximum_fusion.refs_0_
  318.9 27.4 %reduce_weights.1 = bf16[128,896]{1,0:T(8,128)(2,1)} custom-call(bf16[8,128,896]{2,1,0:T(8,128)(2,1)} %maximum_maximum_fusion.refs_0_), custom_call_target="tpu_custom_call" | custom-call | tf_op jit(solution)/shard_map/reduce_weights/pallas_call | solution.py:248
  346.3 0.9 slice.102
  347.9 0.8 slice.100
  349.4 1.7 fusion.16
  351.1 1.7 slice.101
  352.8 1.0 convert_element_type.84
  354.5 0.8 convert_element_type.85
  355.3 1.2 convert_element_type.86
  356.5 1.2 convert_element_type.87
  357.7 1.3 convert_element_type.88
  359.0 1.0 copy.77
  (61 shorter events, 10.1 us)
Async XLA Ops:
  141.1 164.8 %copy-start.7 = (f32[32,256]{1,0:T(8,128)S(1)}, f32[32,256]{1,0:T(8,128)}, u32[]{:S(2)}) copy-start(f32[32,256]{1,0:T(8,128)} %get-tuple-element.72.cos_ref) | copy-start | bytes 98308
  301.2 4.7 %copy-start.3 = (f32[2,384,256]{2,1,0:T(8,128)S(1)}, f32[2,384,256]{2,1,0:T(8,128)}, u32[]{:S(2)}) copy-start(f32[2,384,256]{2,1,0:T(8,128)} %get-tuple-element.48) | copy-start | bytes 2359300
  303.1 4.8 %copy-start = (bf16[2,256,1024]{2,1,0:T(8,128)(2,1)S(1)}, bf16[2,256,1024]{2,1,0:T(8,128)(2,1)}, u32[]{:S(2)}) copy-start(bf16[2,256,1024]{2,1,0:T(8,128)(2,1)} %refs_0_.1) | copy-start | bytes 3145732
  303.1 4.8 %copy-start.9 = (bf16[8,128,896]{2,1,0:T(8,128)(2,1)S(1)}, bf16[8,128,896]{2,1,0:T(8,128)(2,1)}, u32[]{:S(2)}) copy-start(bf16[8,128,896]{2,1,0:T(8,128)(2,1)} %get-tuple-element.44) | copy-start | bytes 5505028
  307.9 2.7 copy-start.10
  307.9 2.8 copy-start.11
  307.9 2.8 copy-start.12
  310.7 1.6 copy-start.1
  318.9 35.6 %copy-start.8 = (bf16[128,1024]{1,0:T(8,128)(2,1)S(1)}, bf16[128,1024]{1,0:T(8,128)(2,1)}, u32[]{:S(2)}) copy-start(bf16[128,1024]{1,0:T(8,128)(2,1)} %get-tuple-element.52) | copy-start | bytes 786436
  318.9 36.4 %copy-start.6 = (bf16[128,2816]{1,0:T(8,128)(2,1)S(1)}, bf16[128,2816]{1,0:T(8,128)(2,1)}, u32[]{:S(2)}) copy-start(bf16[128,2816]{1,0:T(8,128)(2,1)} %get-tuple-element.53) | copy-start | bytes 2162692
  351.1 5.5 %copy-start.5 = (bf16[128,2816]{1,0:T(8,128)(2,1)S(1)}, bf16[128,2816]{1,0:T(8,128)(2,1)}, u32[]{:S(2)}) copy-start(bf16[128,2816]{1,0:T(8,128)(2,1)} %get-tuple-element.54) | copy-start | bytes 2162692
  355.3 2.4 copy-start.4
  356.5 2.5 copy-start.2
where the time goes:
time: 361 us; the launch traced here: 360 us
  Pallas kernels  313 us (87%)
  other arithmetic  21.5 us (6%)
  local copies, waits for them, and re-layouts  20.7 us (6%)
  matrix products  3.74 us (1%)
    pallas_call x1, Pallas kernels, backward(): pl.pallas_call(functools.partial(back_kernel, span, min(512, nk), units,...  160 us
    pallas_call x1, Pallas kernels, forward(): pl.pallas_call(functools.partial(forward_kernel, span, chunk, units, narr...  126 us
    pallas_call x1, Pallas kernels, reduce_weights(): pl.pallas_call(functools.partial(reduce_kernel, units, narr, plan), out_s...  27.4 us

commit v1 on v0

--- a/solution.py
+++ b/solution.py
@@ -1126,6 +1126,96 @@
         name="forward",
     )(tokens, cosine, sine, cond, bl, bs, *weights)
 
+def products_kernel(dqh_ref, dqr_ref, mine_ref, cos_ref, sin_ref, normed_ref, small_ref, tok_ref, res_ref, gain_two_ref, input_ref, out_ref, acc, sums):
+    b = pl.program_id(0)
+    d = tok_ref.shape[-1]
+    nq = tok_ref.shape[1]
+    @pl.when(b == 0)
+    def _():
+        acc[...] = jnp.zeros_like(acc)
+        sums[...] = jnp.zeros_like(sums)
+    cosine, sine = cos_ref[...], -sin_ref[...]
+    mine = mine_ref[0].astype(F32)
+    turned = jnp.concatenate([dqh_ref[0].reshape(96, nq), turn_rows(dqr_ref[0], cosine, sine), turn_rows(mine[:128], cosine, sine), mine[128:],
+                              jnp.zeros((96, nq), F32)], 0)
+    acc[...] += nn(turned.astype(BF16), normed_ref[0])
+    w = small_ref[...].reshape(d, 896)
+    gain = small_ref[:, :, 768:896].reshape(d, 128).astype(F32).T[32:33]
+    back = nt(turned.T.astype(BF16), w)
+    for r in range(0, nq, 128):
+        sl = slice(r, r + 128)
+        x = tok_ref[0, sl, :].astype(F32)
+        scale = lax.rsqrt(jnp.mean(x * x, -1, keepdims=True) + 1e-6)
+        unit = x * scale
+        dn = back[sl]
+        sums[...] += jnp.sum((dn * unit).reshape(16, 8, d), 0)
+        e1 = dn * gain
+        input_ref[0, sl, :] = res_ref[0, sl, :] + scale * (e1 - unit * jnp.mean(e1 * unit, -1, keepdims=True))
+    @pl.when(b == pl.num_programs(0) - 1)
+    def _():
+        total = jnp.sum(sums[...], 0, keepdims=True)
+        for s in range(out_ref.shape[0]):
+            sl = slice(s * 128, s * 128 + 128)
+            out_ref[s, :800, :] = acc[:800, sl].astype(BF16)
+            out_ref[s, 800:, :] = jnp.concatenate([total[:, sl], gain_two_ref[:, sl], jnp.zeros((94, 128), F32)], 0).astype(BF16)
+
+def products(dqh, dqr, mine, cosine, sine, normed, small, tokens, d_resid, gain_two):
+    rows, nq, d = tokens.shape
+    n = small.shape[0]
+    row = lambda a: pl.BlockSpec((1, *a.shape[1:]), lambda b: (b, *([0] * (a.ndim - 1))))
+    one = lambda a: pl.BlockSpec(a.shape, lambda b: (0,) * a.ndim)
+    sd = jax.ShapeDtypeStruct
+    return pl.pallas_call(
+        products_kernel,
+        grid=(rows,),
+        out_shape=[sd(tokens.shape, F32), sd((n, 896, d // n), BF16)],
+        in_specs=[row(dqh), row(dqr), row(mine), one(cosine), one(sine), row(normed), one(small), row(tokens), row(d_resid), one(gain_two)],
+        out_specs=[row(tokens), pl.BlockSpec((n, 896, d // n), lambda b: (0, 0, 0))],
+        scratch_shapes=[pltpu.VMEM((896, d), F32), pltpu.VMEM((8, d), F32)],
+        compiler_params=pltpu.CompilerParams(vmem_limit_bytes=50 << 20),
+        name="products",
+    )(dqh, dqr, mine, cosine, sine, normed, small, tokens, d_resid, gain_two)
+
+def results_kernel(small_ref, out_ref, gate_ref, up_ref, down_ref, qh_ref, qd_ref, kh_ref, kd_ref, vh_ref, vd_ref, g1_ref, g2_ref, o_ref, g_ref, u_ref, d_ref):
+    for src, dst in ((out_ref, o_ref), (gate_ref, g_ref), (up_ref, u_ref), (down_ref, d_ref)):
+        dst[...] = src[...].astype(F32)
+    @pl.when(pl.program_id(0) == 0)
+    def _():
+        flat = small_ref[...].astype(F32)
+        g1_ref[...] = flat[800:801]
+        g2_ref[...] = flat[801:802]
+        across = flat.T.astype(BF16)
+        def pick(lo, hi, n, source):
+            i = lax.broadcasted_iota(jnp.int32, (hi - lo, n), 0)
+            j = lax.broadcasted_iota(jnp.int32, (hi - lo, n), 1)
+            return nn(across[:, lo:hi], jnp.where(i == source(j), 1.0, 0.0).astype(BF16))
+        pair = lambda j: (j & 15) >> 1
+        rank = lambda j: j >> 4
+        qh_ref[...] = pick(0, 128, 96, lambda j: pair(j) * 12 + rank(j) * 2 + (j & 1))
+        qd_ref[...] = pick(0, 512, 384, lambda j: j + 96)
+        kd_ref[...] = pick(384, 640, 128, lambda j: j + 96)
+        vd_ref[...] = pick(512, 768, 128, lambda j: j + 96)
+        kh_ref[...] = pick(640, 896, 32, lambda j: pair(j) * 8 + rank(j) * 2 + (j & 1) + 96)
+        vh_ref[...] = pick(640, 896, 32, lambda j: pair(j) * 8 + rank(j) * 2 + (j & 1) + 100)
+
+def results(small, out, gate, up, down):
+    steps = 2
+    n = small.shape[1]
+    part = lambda a: pl.BlockSpec((a.shape[0] // steps, a.shape[1]), lambda i: (i, 0))
+    one = lambda *s: pl.BlockSpec(s, lambda i: (0, 0))
+    sd = lambda *s: jax.ShapeDtypeStruct(s, F32)
+    shapes = [(n, 96), (n, 384), (n, 32), (n, 128), (n, 32), (n, 128), (1, n), (1, n)]
+    big = (out, gate, up, down)
+    return pl.pallas_call(
+        results_kernel,
+        grid=(steps,),
+        out_shape=[sd(*s) for s in shapes] + [sd(*a.shape) for a in big],
+        in_specs=[one(*small.shape)] + [part(a) for a in big],
+        out_specs=[one(*s) for s in shapes] + [part(a) for a in big],
+        compiler_params=pltpu.CompilerParams(vmem_limit_bytes=40 << 20),
+        name="results",
+    )(small, *big)
+
 HEADS, HDIM, QRANK, KVRANK = 16, 64, 6, 2
 PAIRS = HEADS // 2
 EPSILON = 1e-06
@@ -1221,8 +1311,9 @@
         15: [("own", 8, 0, 1), ("own", 1, 0, 1), ("row", "own", 0), ("own", 3, 0, 1), ("own", 0, 0, 1), ("row", "x", 1), ("last", 1, 0, 1), ("own", 6, 0, 1), ("last", 8, 0, 1), ("last", 0, 0, 1), ("last", 6, 0, 1), ("last", 4, 0, 1), ("last", 5, 0, 1), ("last", 3, 0, 1), ("row", "own", 1), ("end", 0, 0, 1), ("end", 1, 0, 1), ("end", 2, 0, 1), ("end", 3, 0, 1), ("end", 4, 0, 1), ("end", 5, 0, 1), ("end", 6, 0, 1), ("end", 7, 0, 1), ("end", 8, 0, 1), ("results",), ("row", "end", 0), ("row", "end", 1)],
     },
 }
-SMALL_UNITS = [Unit(0, (0, 128), (0, 896), "P", 0)]
-SMALL_PLAN = [("begin", 0, 0, 8), ("core", 0, 0, 8), ("y", 0, 0, 8), ("x", 0, 0, 4), ("own", 0, 0, 1), ("last", 0, 0, 1), ("end", 0, 0, 1)]
+SMALL_UNITS = [Unit(0, (0, 384), (0, 128), "R", 0), Unit(0, (384, 512), (0, 128), "P", 0)]
+SMALL_PLAN = [("begin", 0, 0, 8), ("begin", 1, 0, 8), ("core", 1, 0, 8), ("core", 0, 0, 8), ("x", 0, 0, 4), ("y", 1, 0, 8), ("own", 0, 0, 1), ("x", 1, 0, 4),
+              ("last", 0, 0, 1), ("own", 1, 0, 1), ("last", 1, 0, 1), ("end", 0, 0, 1), ("end", 1, 0, 1)]
 
 
 def reduce_far(arrays):
@@ -1286,7 +1377,10 @@
     if near:
         dqh, dqr, mine, output, d_resid, gain_two_grad, *sums = backward(
             qh, qr, shared, *masks, lse, tokens, heads_out, cotangent, w_out, w_gate, w_up, w_down, gain_two[None, :], REDUCE_UNITS, REDUCE_PLAN, 1)
-        d_resid, gain_two_grad = d_resid.reshape(count, width), gain_two_grad[0]
+        input_grad, small_grad = products(dqh, dqr, mine, cosine, sine, by_row, parts[0], tokens, d_resid, gain_two_grad)
+        small_sum = reduce_weights([small_grad], SMALL_UNITS, SMALL_PLAN, 3)[0]
+        d_qh, d_qd, d_kh, d_kd, d_vh, d_vd, d_g1, d_g2, d_out, d_gate, d_up, d_down = results(small_sum, *sums)
+        return (output, input_grad, d_g1[0], d_qh, d_qd, d_kh, d_kd, d_vh, d_vd, d_out, d_g2[0], d_gate, d_up, d_down)
     else:
         heads_flat = heads_out.reshape(count, width)
 
@@ -1331,7 +1425,7 @@
     small_grad = jnp.concatenate([small_grad, gain_one_grad[:, None], gain_two_grad[:, None], jnp.zeros((width, 94), F32)], 1).astype(BF16)
 
     small_grad = small_grad.reshape(nseq, -1, 896)
-    small_sum = reduce_weights([small_grad], SMALL_UNITS, SMALL_PLAN, 3)[0] if near else reduce_far([small_grad])[0]
+    small_sum = reduce_far([small_grad])[0]
     small_sum = small_sum.astype(F32)
     out_sum, gate_sum, up_sum, down_sum = [g.astype(F32) for g in sums]
     key_value = head_columns(small_sum[:, 736:800], 4)

time: 361 us -> 343 us (0.950)
  other arithmetic: 21.5 us -> 5.89 us
  Pallas kernels: 313 us -> 321 us
  local copies, waits for them, and re-layouts: 20.7 us -> 14.6 us
  matrix products: 3.74 us -> 0 us
    pallas_call x0 -> x2, Pallas kernels: none -> 9.78 us  [the longest x1 6.93 us: products(): pl.pallas_call(products_kernel, grid=(rows,), out_shape=[sd(tokens.shape,...]
    slice x10 -> x1, local copies, waits for them, and re-layouts: 8.63 us -> 1.08 us  [per_device(): gain_two = small[:, 801].astype(F32)]
    convert_element_type x6 -> x0, other arithmetic: 6.7 us -> none  [the longest x4 4.49 us: per_device(): out_sum, gate_sum, up_sum, down_sum = [g.astype(F32) for g in sums]]
    unnamed x29 -> x33, local copies, waits for them, and re-layouts: 1.89 us -> 7.86 us
    dot_general x2 -> x0, matrix products: 3.74 us -> none  [dot(): lax.dot_general(a, b, ((ca, cb), ((), ())), preferred_element_type=F32)]
where the time goes in v1:
time: 343 us; the launch traced here: 342 us
  Pallas kernels  321 us (94%)
  local copies, waits for them, and re-layouts  14.6 us (4%)
  other arithmetic  5.89 us (2%)
    pallas_call x1, Pallas kernels, backward(): pl.pallas_call(functools.partial(back_kernel, span, min(512, nk), units,...  160 us
    pallas_call x1, Pallas kernels, forward(): pl.pallas_call(functools.partial(forward_kernel, span, chunk, units, narr...  126 us
    pallas_call x1, Pallas kernels, reduce_weights(): pl.pallas_call(functools.partial(reduce_kernel, units, narr, plan), out_s...  25.2 us
    unnamed x33, local copies, waits for them, and re-layouts  7.86 us
    pallas_call x1, Pallas kernels, products(): pl.pallas_call(products_kernel, grid=(rows,), out_shape=[sd(tokens.shape,...  6.93 us

profile of v1, /device:TPU:0, one launch (start us, length us, event | category | flops | bytes accessed | tf_op | source)
XLA Modules:
  0.0 342.3 jit_solution(7573805327971060216)
XLA Ops:
  0.7 0.8 pad_add_fusion
  1.6 0.5 slice.19
  2.1 0.6 fusion
  2.7 0.1 multiply_reduce_fusion
  2.9 0.7 fusion.2
  3.6 0.7 broadcast_in_dim.16
  4.3 1.3 compare_select_fusion
  5.7 0.7 pad_maximum_fusion
  6.4 0.1 copy.40
  6.5 0.8 copy.37
  7.4 0.8 copy.41
  8.2 0.8 copy.42
  9.0 0.8 multiply_sine_fusion
  9.8 1.1 concatenate.11
  10.9 0.7 pad.4.refs_0_
  11.6 125.7 %forward.1 = (bf16[2,256,1024]{2,1,0:T(8,128)(2,1)}, f32[2,8,12,256]{3,2,1,0:T(8,128)}, f32[2,384,256]{2,1,0:T(8,128)}, bf16[8,2,320,256]{3,2,1,0:T(8,128)(2,1)}...) custom-call(bf16[2,256,1024]{2,1,0:T(8,128)(2,1)} %tok_ref.3, ...), custom_call_target="tpu_custom_call" | custom-call | tf_op jit(solution)/shard_map/forward/pallas_call | solution.py:1117
  137.3 1.1 slice.22
  138.4 0.1 copy.47
  138.6 0.6 bitcast_convert_fusion.refs_7_
  139.2 160.3 %backward.1 = (f32[2,8,12,256]{3,2,1,0:T(8,128)}, f32[2,384,256]{2,1,0:T(8,128)}, bf16[2,320,256]{2,1,0:T(8,128)(2,1)}, bf16[2,256,1024]{2,1,0:T(8,128)(2,1)}, f...) custom-call(f32[2,8,12,256]{3,2,1,0:T(8,128)} %get-tuple-element.49., ...), custom_call_target="tpu_custom_call" | custom-call | tf_op jit(solution)/shard_map/backward/pallas_call | solution.py:867
  299.6 1.1 copy-done.3
  300.7 1.0 copy-done.7
  301.7 0.9 copy-done.10
  302.6 0.7 copy-done.12
  303.3 6.9 %products.1 = (f32[2,256,1024]{2,1,0:T(8,128)}, bf16[8,896,128]{2,1,0:T(8,128)(2,1)}) custom-call(f32[2,8,12,256]{3,2,1,0:T(8,128)S(1)} %copy-done.10, f32[2,384,256]{2,1,0:T(8,128)S(1)} %copy-done.3, bf16[2,320,256]{2,1,0:T(8,128)(2,1)S(1)} %copy-done.7, f32[32,256]{1,0:T(8,128)S(1)} %copy-done.9, f32[32,256]{1,0:T(8,128)S(1)} %copy-done.8, ...), custom_call_target="tpu_custom_call" | custom-call | tf_op jit(solution)/shard_map/products/pallas_call | solution.py:1168
  310.2 25.2 %reduce_weights.1.small_ref = bf16[896,128]{1,0:T(8,128)(2,1)} custom-call(bf16[8,896,128]{2,1,0:T(8,128)(2,1)} %get-tuple-element.67.refs_0_), custom_call_target="tpu_custom_call" | custom-call | tf_op jit(solution)/shard_map/reduce_weights/pallas_call | solution.py:248
  335.5 0.9 copy-done.2
  336.4 2.9 results.1
  339.2 0.7 copy.45
  339.9 0.7 copy.46
  340.6 0.7 copy.44
  341.3 1.0 copy.49
  (29 shorter events, 0.4 us)
Async XLA Ops:
  139.2 160.3 %copy-start = (bf16[2,256,1024]{2,1,0:T(8,128)(2,1)S(1)}, bf16[2,256,1024]{2,1,0:T(8,128)(2,1)}, u32[]{:S(2)}) copy-start(bf16[2,256,1024]{2,1,0:T(8,128)(2,1)} %tok_ref.3) | copy-start | bytes 3145732
  139.2 160.4 %copy-start.1 = (bf16[2,256,1024]{2,1,0:T(8,128)(2,1)S(1)}, bf16[2,256,1024]{2,1,0:T(8,128)(2,1)}, u32[]{:S(2)}) copy-start(bf16[2,256,1024]{2,1,0:T(8,128)(2,1)} %get-tuple-element.63.normed_ref) | copy-start | bytes 3145732
  139.2 160.4 %copy-start.8 = (f32[32,256]{1,0:T(8,128)S(1)}, f32[32,256]{1,0:T(8,128)}, u32[]{:S(2)}) copy-start(f32[32,256]{1,0:T(8,128)} %get-tuple-element.112.sin_ref) | copy-start | bytes 98308
  139.2 160.4 %copy-start.9 = (f32[32,256]{1,0:T(8,128)S(1)}, f32[32,256]{1,0:T(8,128)}, u32[]{:S(2)}) copy-start(f32[32,256]{1,0:T(8,128)} %get-tuple-element.113.cos_ref) | copy-start | bytes 98308
  299.6 1.1 copy-start.3
  300.7 1.0 copy-start.7
  301.7 0.9 copy-start.10
  302.6 0.7 copy-start.12
  303.3 32.1 %copy-start.6 = (bf16[352,1024]{1,0:T(8,128)(2,1)S(1)}, bf16[352,1024]{1,0:T(8,128)(2,1)}, u32[]{:S(2)}) copy-start(bf16[352,1024]{1,0:T(8,128)(2,1)} %get-tuple-element.71.down_ref) | copy-start | bytes 2162692
  310.2 25.2 %copy-start.4 = (bf16[128,2816]{1,0:T(8,128)(2,1)S(1)}, bf16[128,2816]{1,0:T(8,128)(2,1)}, u32[]{:S(2)}) copy-start(bf16[128,2816]{1,0:T(8,128)(2,1)} %get-tuple-element.69.gate_ref) | copy-start | bytes 2162692
  310.2 25.2 %copy-start.5 = (bf16[128,2816]{1,0:T(8,128)(2,1)S(1)}, bf16[128,2816]{1,0:T(8,128)(2,1)}, u32[]{:S(2)}) copy-start(bf16[128,2816]{1,0:T(8,128)(2,1)} %get-tuple-element.70.up_ref) | copy-start | bytes 2162692
  310.2 25.2 %copy-start.11 = (bf16[128,1024]{1,0:T(8,128)(2,1)S(1)}, bf16[128,1024]{1,0:T(8,128)(2,1)}, u32[]{:S(2)}) copy-start(bf16[128,1024]{1,0:T(8,128)(2,1)} %get-tuple-element.68.out_ref) | copy-start | bytes 786436
  335.4 0.9 copy-start.2
  336.4 4.9 %copy-start.13 = (bf16[2,256,1024]{2,1,0:T(8,128)(2,1)S(1)}, bf16[2,256,1024]{2,1,0:T(8,128)(2,1)}, u32[]{:S(2)}) copy-start(bf16[2,256,1024]{2,1,0:T(8,128)(2,1)} %get-tuple-element.134) | copy-start | bytes 3145732

commit v2 on v1

--- a/solution.py
+++ b/solution.py
@@ -1035,7 +1035,7 @@
         out += [a * cosine - b * sine, b * cosine + a * sine]
     return jnp.concatenate(out, 0)
 
-def project(me, span, tok_ref, small_ref, cos_ref, sin_ref, normed_ref, qh_ref, qr_ref, shared_ref, b):
+def project(me, span, tok_ref, small_ref, cos_ref, sin_ref, normed_ref, qh_ref, qr_ref, shared_ref, gain_ref, b):
     nq = 2 * span
     d = tok_ref.shape[-1]
     gains = small_ref[:, :, 768:896].reshape(d, 128).astype(F32).T
@@ -1043,6 +1043,7 @@
     unit = x * lax.rsqrt(jnp.mean(x * x, -1, keepdims=True) + 1e-6)
     normed = (unit * gains[32:33]).astype(BF16)
     normed_ref[b] = normed
+    gain_ref[...] = gains[33:34]
     w = small_ref[...].reshape(d, 896)
     f = nn(normed, w).T
     qh_ref[b] = f[:96].reshape(PAIRS, 12, nq)
@@ -1053,14 +1054,14 @@
 
 def forward_kernel(span, chunk, units, narr, plan, tok_ref, cos_ref, sin_ref, cond_ref, bl_ref, bs_ref, *refs):
     ins = refs[:narr]
-    normed_ref, qh_ref, qr_ref, shared_out, o_ref, lse_ref = refs[narr:narr + 6]
-    outs = refs[narr + 6:2 * narr + 6]
-    shared_ref, small, saved, dl, ds, hl, hs, s1, s2, rzs, rzr, rxs, rxr = refs[2 * narr + 6:2 * narr + 19]
+    normed_ref, qh_ref, qr_ref, shared_out, o_ref, lse_ref, gain_ref = refs[narr:narr + 7]
+    outs = refs[narr + 7:2 * narr + 7]
+    shared_ref, small, saved, dl, ds, hl, hs, s1, s2, rzs, rzr, rxs, rxr = refs[2 * narr + 7:2 * narr + 20]
     small_out, outs = outs[0], (small, *outs[1:])
     me = Place()
     b, p = pl.program_id(0), pl.program_id(1)
     step = b * PAIRS + p
-    gat = Gather(me, units, ins, outs, refs[2 * narr + 19:])
+    gat = Gather(me, units, ins, outs, refs[2 * narr + 20:])
     saves = (pltpu.make_async_copy(small, small_out, saved.at[0]), pltpu.make_async_copy(shared_ref, shared_out, saved.at[1]))
     row = RowsGather(me, shared_ref, rzs, rzr, rxs, rxr)
 
@@ -1070,7 +1071,7 @@
                 getattr(row, it[1])(it[2])
             elif it[0] == "project":
                 for r in range(tok_ref.shape[0]):
-                    project(me, span, tok_ref, small, cos_ref, sin_ref, normed_ref, qh_ref, qr_ref, shared_ref, r)
+                    project(me, span, tok_ref, small, cos_ref, sin_ref, normed_ref, qh_ref, qr_ref, shared_ref, gain_ref, r)
             elif it[0] == "local":
                 for a in range(narr):
                     gat.local(a).start()
@@ -1118,11 +1119,11 @@
         functools.partial(forward_kernel, span, chunk, units, narr, plan),
         grid=(rows, PAIRS),
         out_shape=[sd((rows, nq, width), BF16), sd((rows, PAIRS, 12, nq), F32), sd((rows, 384, nq), F32), sd((n, rows, 320, nq), BF16),
-                   sd((rows, nq, width), BF16), sd((rows, nq, 128), F32)] + [sd((n, *a.shape), a.dtype) for a in weights],
+                   sd((rows, nq, width), BF16), sd((rows, nq, 128), F32), sd((1, width), F32)] + [sd((n, *a.shape), a.dtype) for a in weights],
         in_specs=[whole, whole, whole, pl.BlockSpec((1, nk), lambda b, p: (0, 0)), full(1, nk), full(1, nk)] + [far] * narr,
-        out_specs=[whole, whole, whole, far, pl.BlockSpec((1, nq, 128), lambda b, p: (b, 0, p)), full(nq, 128)] + [far] * narr,
+        out_specs=[whole, whole, whole, far, pl.BlockSpec((1, nq, 128), lambda b, p: (b, 0, p)), full(nq, 128), whole] + [far] * narr,
         scratch_shapes=scratch,
-        compiler_params=pltpu.CompilerParams(collective_id=cid, has_side_effects=True, vmem_limit_bytes=56 << 20),
+        compiler_params=pltpu.CompilerParams(collective_id=cid, has_side_effects=True, vmem_limit_bytes=62 << 20),
         name="forward",
     )(tokens, cosine, sine, cond, bl, bs, *weights)
 
@@ -1172,7 +1173,7 @@
         in_specs=[row(dqh), row(dqr), row(mine), one(cosine), one(sine), row(normed), one(small), row(tokens), row(d_resid), one(gain_two)],
         out_specs=[row(tokens), pl.BlockSpec((n, 896, d // n), lambda b: (0, 0, 0))],
         scratch_shapes=[pltpu.VMEM((896, d), F32), pltpu.VMEM((8, d), F32)],
-        compiler_params=pltpu.CompilerParams(vmem_limit_bytes=50 << 20),
+        compiler_params=pltpu.CompilerParams(vmem_limit_bytes=62 << 20),
         name="products",
     )(dqh, dqr, mine, cosine, sine, normed, small, tokens, d_resid, gain_two)
 
@@ -1191,12 +1192,12 @@
             return nn(across[:, lo:hi], jnp.where(i == source(j), 1.0, 0.0).astype(BF16))
         pair = lambda j: (j & 15) >> 1
         rank = lambda j: j >> 4
-        qh_ref[...] = pick(0, 128, 96, lambda j: pair(j) * 12 + rank(j) * 2 + (j & 1))
+        qh_ref[...] = pick(0, 128, 96, lambda j: pair(j) * 12 + rank(j) * 2 + (j & 1)).T
         qd_ref[...] = pick(0, 512, 384, lambda j: j + 96)
         kd_ref[...] = pick(384, 640, 128, lambda j: j + 96)
         vd_ref[...] = pick(512, 768, 128, lambda j: j + 96)
-        kh_ref[...] = pick(640, 896, 32, lambda j: pair(j) * 8 + rank(j) * 2 + (j & 1) + 96)
-        vh_ref[...] = pick(640, 896, 32, lambda j: pair(j) * 8 + rank(j) * 2 + (j & 1) + 100)
+        kh_ref[...] = pick(640, 896, 32, lambda j: pair(j) * 8 + rank(j) * 2 + (j & 1) + 96).T
+        vh_ref[...] = pick(640, 896, 32, lambda j: pair(j) * 8 + rank(j) * 2 + (j & 1) + 100).T
 
 def results(small, out, gate, up, down):
     steps = 2
@@ -1204,7 +1205,7 @@
     part = lambda a: pl.BlockSpec((a.shape[0] // steps, a.shape[1]), lambda i: (i, 0))
     one = lambda *s: pl.BlockSpec(s, lambda i: (0, 0))
     sd = lambda *s: jax.ShapeDtypeStruct(s, F32)
-    shapes = [(n, 96), (n, 384), (n, 32), (n, 128), (n, 32), (n, 128), (1, n), (1, n)]
+    shapes = [(96, n), (n, 384), (32, n), (n, 128), (32, n), (n, 128), (1, n), (1, n)]
     big = (out, gate, up, down)
     return pl.pallas_call(
         results_kernel,
@@ -1212,9 +1213,64 @@
         out_shape=[sd(*s) for s in shapes] + [sd(*a.shape) for a in big],
         in_specs=[one(*small.shape)] + [part(a) for a in big],
         out_specs=[one(*s) for s in shapes] + [part(a) for a in big],
-        compiler_params=pltpu.CompilerParams(vmem_limit_bytes=40 << 20),
+        compiler_params=pltpu.CompilerParams(vmem_limit_bytes=62 << 20),
         name="results",
     )(small, *big)
+
+def prepare_kernel(n, span, order, lengths, inverse, qh, qd, kh, kd, vh, vd, g1, g2, small_ref, cond_ref, bl_ref, bs_ref, cos_ref, sin_ref):
+    me = lax.axis_index("seq")
+    rows = bl_ref.shape[0]
+    lane = lax.broadcasted_iota(jnp.int32, (1, span), 1)
+    own = order[0, me]
+    for i in range(n):
+        j = lax.rem(me + i, n)
+        sl = slice(i * span, (i + 1) * span)
+        low = order[0, j]
+        chosen = low < own
+        sel = jnp.where(chosen, low, order[1, j])
+        cond_ref[:, sl] = jnp.full((1, span), jnp.where(chosen, 1.0, 0.0), F32)
+        for b in range(rows):
+            bl_ref[b, :, sl] = jnp.where(lane + low * span < lengths[b], 0.0, NEG)
+            bs_ref[b, :, sl] = jnp.where(lane + sel * span < lengths[b], 0.0, NEG)
+    for k in range(2):
+        angle = inverse[...] * (lane + order[k, me] * span).astype(F32)
+        sl = slice(k * span, (k + 1) * span)
+        cos_ref[:, sl] = jnp.cos(angle)
+        sin_ref[:, sl] = jnp.sin(angle)
+    def place(ref, target, turned=False):
+        value = ref[...].astype(F32).T.astype(BF16) if turned else ref[...]
+        i = lax.broadcasted_iota(jnp.int32, (value.shape[1], 896), 0)
+        j = lax.broadcasted_iota(jnp.int32, (value.shape[1], 896), 1)
+        return nn(value, jnp.where(j == target(i), 1.0, 0.0).astype(BF16))
+    pair = lambda i: (i & 15) >> 1
+    rank = lambda i: i >> 4
+    out = place(qh, lambda i: pair(i) * 12 + rank(i) * 2 + (i & 1), True) + place(qd, lambda i: i + 96)
+    out = out + place(kd, lambda i: i + 480) + place(vd, lambda i: i + 608)
+    out = out + place(kh, lambda i: 736 + pair(i) * 8 + rank(i) * 2 + (i & 1), True)
+    out = out + place(vh, lambda i: 740 + pair(i) * 8 + rank(i) * 2 + (i & 1), True)
+    d = out.shape[0]
+    eye = lax.broadcasted_iota(jnp.int32, (d, d), 0) == lax.broadcasted_iota(jnp.int32, (d, d), 1)
+    at = lax.broadcasted_iota(jnp.int32, (d, 896), 1)
+    for ref, column in ((g1, 800), (g2, 801)):
+        gain = jnp.sum(jnp.where(eye, ref[...].astype(F32), 0.0), 1, keepdims=True)
+        out = jnp.where(at == column, gain, out)
+    small_ref[...] = out.astype(BF16)
+
+def prepare(span_order, lengths, inverse, query_heads, query_dims, key_heads, key_dims, value_heads, value_dims, gain_one, gain_two, slots):
+    n, rows = span_order.shape[0], lengths.shape[0]
+    span = slots // 2
+    d = query_heads.shape[0]
+    smem = pl.BlockSpec(memory_space=pltpu.SMEM)
+    whole = pl.BlockSpec(memory_space=pltpu.VMEM)
+    sd = jax.ShapeDtypeStruct
+    return pl.pallas_call(
+        functools.partial(prepare_kernel, n, span),
+        out_shape=[sd((d, 896), BF16), sd((1, n * span), F32), sd((rows, 1, n * span), F32), sd((rows, 1, n * span), F32), sd((32, slots), F32), sd((32, slots), F32)],
+        in_specs=[smem, smem] + [whole] * 9,
+        out_specs=[whole] * 6,
+        compiler_params=pltpu.CompilerParams(vmem_limit_bytes=62 << 20),
+        name="prepare",
+    )(span_order.T, lengths, inverse, query_heads.T, query_dims, key_heads.T, key_dims, value_heads.T, value_dims, gain_one[None, :], gain_two[None, :])
 
 HEADS, HDIM, QRANK, KVRANK = 16, 64, 6, 2
 PAIRS = HEADS // 2
@@ -1266,17 +1322,15 @@
     Unit(3, (0, 128), (0, 1408), "R", 0), Unit(3, (0, 128), (1408, 1408), "P", 0),
     Unit(4, (0, 176), (0, 1024), "P", 1), Unit(4, (176, 176), (0, 1024), "P", 1)]
 GATHER_PLAN = {
-    "first": [("local",), ("begin", 0, 1, 3), ("begin", 1, 1, 3), ("z", 0, 1, 3), ("x", 0, 0, 4), ("begin", 3, 1, 3), ("y", 0, 1, 7), ("begin", 7, 1, 3), ("begin", 2, 1, 3), ("z", 1, 1, 3), ("got", 0, 1, 7), ("x", 1, 0, 4), ("begin", 6, 1, 3), ("z", 3, 1, 3), ("project",), ("z", 2, 1, 3), ("x", 3, 0, 4), ("row", "begin", 0), ("row", "begin", 1), ("x", 2, 0, 4), ("z", 7, 1, 3), ("row", "z", 0), ("z", 6, 1, 3), ("row", "x", 0), ("y", 3, 4, 4), ("y", 2, 1, 3), ("begin", 5, 1, 3), ("begin", 4, 1, 3), ("y", 7, 1, 3)],
+    "first": [("local",), ("begin", 0, 1, 3), ("begin", 5, 1, 3), ("z", 0, 1, 3), ("x", 0, 0, 4), ("begin", 3, 1, 3), ("y", 0, 1, 7), ("begin", 2, 1, 3), ("got", 0, 1, 7), ("z", 5, 1, 3), ("begin", 7, 1, 3), ("project",), ("row", "begin", 0), ("z", 3, 1, 3), ("x", 5, 0, 4), ("z", 7, 1, 3), ("y", 5, 4, 4), ("z", 2, 1, 3), ("begin", 6, 1, 3), ("row", "z", 0), ("x", 3, 0, 4), ("row", "begin", 1), ("begin", 1, 1, 3), ("x", 7, 0, 4), ("row", "x", 0), ("z", 6, 1, 3), ("y", 7, 1, 3), ("y", 2, 1, 3)],
     "steps": {
-        2: [("x", 6, 0, 4), ("y", 1, 1, 3), ("y", 3, 1, 3), ("row", "z", 1)],
-        5: [("z", 5, 1, 3), ("y", 1, 4, 4)],
-        6: [("x", 7, 0, 4)],
-        7: [("y", 2, 4, 4), ("row", "x", 1)],
-        10: [("z", 4, 1, 3), ("x", 5, 0, 4)],
-        12: [("y", 7, 4, 4), ("y", 6, 1, 3)],
-        13: [("y", 6, 4, 4), ("y", 5, 1, 3)],
-        14: [("x", 4, 0, 4)],
-        15: [("y", 5, 4, 4), ("got", 1, 1, 7), ("got", 2, 1, 7), ("got", 3, 1, 7), ("got", 4, 1, 7), ("got", 5, 1, 7), ("got", 6, 1, 7), ("got", 7, 1, 7), ("locals",), ("sent", 0, 1, 7), ("sent", 1, 1, 7), ("sent", 2, 1, 7), ("sent", 3, 1, 7), ("sent", 4, 1, 7), ("sent", 5, 1, 7), ("sent", 6, 1, 7), ("sent", 7, 1, 7), ("row", "end", 0), ("row", "end", 1)],
+        3: [("y", 3, 1, 3), ("y", 5, 1, 3), ("y", 7, 4, 4), ("row", "z", 1), ("x", 2, 0, 4)],
+        4: [("begin", 4, 1, 3)],
+        6: [("z", 1, 1, 3), ("y", 3, 4, 4)],
+        7: [("row", "x", 1), ("x", 6, 0, 4)],
+        11: [("y", 1, 1, 3), ("z", 4, 1, 3), ("x", 1, 0, 4), ("y", 6, 1, 3)],
+        12: [("y", 2, 4, 4)],
+        15: [("y", 1, 4, 4), ("x", 4, 0, 4), ("y", 6, 4, 4), ("got", 1, 1, 7), ("got", 2, 1, 7), ("got", 3, 1, 7), ("got", 4, 1, 7), ("got", 5, 1, 7), ("got", 6, 1, 7), ("got", 7, 1, 7), ("locals",), ("sent", 0, 1, 7), ("sent", 1, 1, 7), ("sent", 2, 1, 7), ("sent", 3, 1, 7), ("sent", 4, 1, 7), ("sent", 5, 1, 7), ("sent", 6, 1, 7), ("sent", 7, 1, 7), ("row", "end", 0), ("row", "end", 1)],
     },
 }
 REDUCE_UNITS = [
@@ -1332,34 +1386,38 @@
     nseq = span_order.shape[0]
     nk = nseq * span
     me = lax.axis_index("seq")
-    key_value_heads = pair_columns(jnp.concatenate([key_heads, value_heads], 1), 4)
-    small = jnp.concatenate([pair_columns(query_heads, QRANK), query_dims, key_dims, value_dims, key_value_heads, attn_gain[:, None], ffn_gain[:, None]], 1)
-    small = jnp.pad(small, ((0, 0), (0, 896 - small.shape[1])))
-    offsets = jnp.arange(span, dtype=jnp.int32)
-    spans = jnp.concatenate([span_order, span_order], 0)
-    spans = lax.dynamic_slice_in_dim(spans, me, nseq, 0)
-    local_pos = (spans[0][:, None] * span + offsets[None, :]).reshape(-1)
-    cosine, sine = rotation(local_pos)
-    chosen = spans[:, 0] < spans[0, 0]
-    low_pos = (spans[:, 0][:, None] * span + offsets[None, :]).reshape(1, nk)
-    sel_pos = (jnp.where(chosen, spans[:, 0], spans[:, 1])[:, None] * span + offsets[None, :]).reshape(1, nk)
-    cond = jnp.repeat(chosen.astype(F32), span).reshape(1, nk)
-    low_bias = jnp.where(low_pos < lengths[:, None], 0.0, NEG)[:, None, :]
-    sel_bias = jnp.where(sel_pos < lengths[:, None], 0.0, NEG)[:, None, :]
-
+    flat = tokens.reshape(count, width).astype(F32)
+    if near:
+        inverse = jnp.exp(jnp.arange(HDIM // 2).astype(F32) * (-math.log(10000.0) / (HDIM // 2)))[:, None]
+        small, cond, low_bias, sel_bias, cosine, sine = prepare(span_order, lengths, inverse, query_heads, query_dims, key_heads, key_dims,
+                                                                value_heads, value_dims, attn_gain, ffn_gain, slots)
+    else:
+        key_value_heads = pair_columns(jnp.concatenate([key_heads, value_heads], 1), 4)
+        small = jnp.concatenate([pair_columns(query_heads, QRANK), query_dims, key_dims, value_dims, key_value_heads, attn_gain[:, None], ffn_gain[:, None]], 1)
+        small = jnp.pad(small, ((0, 0), (0, 896 - small.shape[1])))
+        offsets = jnp.arange(span, dtype=jnp.int32)
+        spans = jnp.concatenate([span_order, span_order], 0)
+        spans = lax.dynamic_slice_in_dim(spans, me, nseq, 0)
+        local_pos = (spans[0][:, None] * span + offsets[None, :]).reshape(-1)
+        cosine, sine = rotation(local_pos)
+        chosen = spans[:, 0] < spans[0, 0]
+        low_pos = (spans[:, 0][:, None] * span + offsets[None, :]).reshape(1, nk)
+        sel_pos = (jnp.where(chosen, spans[:, 0], spans[:, 1])[:, None] * span + offsets[None, :]).reshape(1, nk)
+        cond = jnp.repeat(chosen.astype(F32), span).reshape(1, nk)
+        low_bias = jnp.where(low_pos < lengths[:, None], 0.0, NEG)[:, None, :]
+        sel_bias = jnp.where(sel_pos < lengths[:, None], 0.0, NEG)[:, None, :]
     masks = (cond, low_bias, sel_bias)
-    flat = tokens.reshape(count, width).astype(F32)
     weights = [small, out_proj, gate_proj, up_proj, down_proj]
     if near:
-        by_row, qh, qr, shared, heads_out, lse, *parts = forward(tokens, cosine, sine, *masks, weights, GATHER_UNITS, GATHER_PLAN, 0)
+        by_row, qh, qr, shared, heads_out, lse, gain_two, *parts = forward(tokens, cosine, sine, *masks, weights, GATHER_UNITS, GATHER_PLAN, 0)
     else:
         parts = [lax.all_gather(a, "seq", axis=0) for a in weights]
     small, w_out, w_gate, w_up, w_down = [p.reshape(-1, p.shape[-1]) for p in parts]
     w_qkv = small[:, :800]
     gain_one = small[:, 800].astype(F32)
-    gain_two = small[:, 801].astype(F32)
     normed_full, unit_one, scale_one = rms_forward(flat, gain_one)
     if not near:
+        gain_two = small[:, 801].astype(F32)
         by_row = normed_full.astype(BF16).reshape(rows, slots, width)
         factors = jnp.stack([dot(w_qkv, by_row[b], (0,), (1,)) for b in range(rows)])
         qh = factors[:, :96].reshape(rows, PAIRS, 12, slots)
@@ -1376,11 +1434,11 @@
         heads_out, lse = attend(qh, qr, *factors, *masks)
     if near:
         dqh, dqr, mine, output, d_resid, gain_two_grad, *sums = backward(
-            qh, qr, shared, *masks, lse, tokens, heads_out, cotangent, w_out, w_gate, w_up, w_down, gain_two[None, :], REDUCE_UNITS, REDUCE_PLAN, 1)
+            qh, qr, shared, *masks, lse, tokens, heads_out, cotangent, w_out, w_gate, w_up, w_down, gain_two, REDUCE_UNITS, REDUCE_PLAN, 1)
         input_grad, small_grad = products(dqh, dqr, mine, cosine, sine, by_row, parts[0], tokens, d_resid, gain_two_grad)
         small_sum = reduce_weights([small_grad], SMALL_UNITS, SMALL_PLAN, 3)[0]
         d_qh, d_qd, d_kh, d_kd, d_vh, d_vd, d_g1, d_g2, d_out, d_gate, d_up, d_down = results(small_sum, *sums)
-        return (output, input_grad, d_g1[0], d_qh, d_qd, d_kh, d_kd, d_vh, d_vd, d_out, d_g2[0], d_gate, d_up, d_down)
+        return (output, input_grad, d_g1[0], d_qh.T, d_qd, d_kh.T, d_kd, d_vh.T, d_vd, d_out, d_g2[0], d_gate, d_up, d_down)
     else:
         heads_flat = heads_out.reshape(count, width)
 

time: 343 us -> 321 us (0.936)
  local copies, waits for them, and re-layouts: 14.6 us -> 0.98 us
  other arithmetic: 5.89 us -> 0.62 us
    unnamed x33 -> x3, local copies, waits for them, and re-layouts: 7.86 us -> 0.98 us
    pallas_call x1, Pallas kernels: 160 us -> 155 us  [backward(): pl.pallas_call(functools.partial(back_kernel, span, min(512, nk), units,...]
where the time goes in v2:
time: 321 us
  Pallas kernels  319 us (99%)
    pallas_call x1, Pallas kernels, backward(): pl.pallas_call(functools.partial(back_kernel, span, min(512, nk), units,...  155 us
    pallas_call x1, Pallas kernels, forward(): pl.pallas_call(functools.partial(forward_kernel, span, chunk, units, narr...  124 us
    pallas_call x1, Pallas kernels, reduce_weights(): pl.pallas_call(functools.partial(reduce_kernel, units, narr, plan), out_s...  25.4 us
    pallas_call x1, Pallas kernels, products(): pl.pallas_call(products_kernel, grid=(rows,), out_shape=[sd(tokens.shape,...  7.77 us

profile of v2, /device:TPU:0, one launch (start us, length us, event | category | flops | bytes accessed | tf_op | source)
XLA Modules:
  0.0 321.0 jit_solution(864104388245478260)
XLA Ops:
  0.6 0.6 multiply_exponential_fusion.inverse
  1.3 2.3 prepare.1
  3.6 124.3 %forward.1 = (bf16[2,256,1024]{2,1,0:T(8,128)(2,1)}, f32[2,8,12,256]{3,2,1,0:T(8,128)}, f32[2,384,256]{2,1,0:T(8,128)}, bf16[8,2,320,256]{3,2,1,0:T(8,128)(2,1)}...) custom-call(bf16[2,256,1024]{2,1,0:T(8,128)(2,1)} %tok_ref.3, ...), custom_call_target="tpu_custom_call" | custom-call | tf_op jit(solution)/shard_map/forward/pallas_call | solution.py:1118
  127.9 154.6 %backward.1 = (f32[2,8,12,256]{3,2,1,0:T(8,128)}, f32[2,384,256]{2,1,0:T(8,128)}, bf16[2,320,256]{2,1,0:T(8,128)(2,1)}, bf16[2,256,1024]{2,1,0:T(8,128)(2,1)}, f...) custom-call(f32[2,8,12,256]{3,2,1,0:T(8,128)} %get-tuple-element.62., ...), custom_call_target="tpu_custom_call" | custom-call | tf_op jit(solution)/shard_map/backward/pallas_call | solution.py:867
  282.4 7.8 %products.1 = (f32[2,256,1024]{2,1,0:T(8,128)}, bf16[8,896,128]{2,1,0:T(8,128)(2,1)}) custom-call(f32[2,8,12,256]{3,2,1,0:T(8,128)} %get-tuple-element.73.dqh_ref, f32[2,384,256]{2,1,0:T(8,128)} %get-tuple-element.74.dqr_ref, bf16[2,320,256]{2,1,0:T(8,128)(2,1)} %get-tuple-element.75.mine_ref, f32[32,256]{1,0:T(8,128)} %get-tuple-element.56.cos_ref, ...), custom_call_target="tpu_custom_call" | custom-call | tf_op jit(solution)/shard_map/products/pallas_call | solution.py:1169
  290.2 0.0 copy-start
  290.2 25.4 %reduce_weights.1.small_ref = bf16[896,128]{1,0:T(8,128)(2,1)} custom-call(bf16[8,896,128]{2,1,0:T(8,128)(2,1)} %get-tuple-element.81.refs_0_), custom_call_target="tpu_custom_call" | custom-call | tf_op jit(solution)/shard_map/reduce_weights/pallas_call | solution.py:248
  315.6 4.4 %results.1 = (f32[96,128]{1,0:T(8,128)}, f32[128,384]{1,0:T(8,128)}, f32[32,128]{1,0:T(8,128)}, f32[128,128]{1,0:T(8,128)}, f32[32,128]{1,0:T(8,128)}, /*index=5...) custom-call(bf16[896,128]{1,0:T(8,128)(2,1)} %reduce_weights.1.small, ...), custom_call_target="tpu_custom_call" | custom-call | tf_op jit(solution)/shard_map/results/pallas_call | solution.py:1210
  320.1 0.0 copy-done
  320.1 1.0 copy.31
Async XLA Ops:
  290.2 29.8 %copy-start = (bf16[2,256,1024]{2,1,0:T(8,128)(2,1)S(1)}, bf16[2,256,1024]{2,1,0:T(8,128)(2,1)}, u32[]{:S(2)}) copy-start(bf16[2,256,1024]{2,1,0:T(8,128)(2,1)} %get-tuple-element.112) | copy-start | bytes 3145732

commit v3 on v2

--- a/solution.py
+++ b/solution.py
@@ -1365,8 +1365,8 @@
         15: [("own", 8, 0, 1), ("own", 1, 0, 1), ("row", "own", 0), ("own", 3, 0, 1), ("own", 0, 0, 1), ("row", "x", 1), ("last", 1, 0, 1), ("own", 6, 0, 1), ("last", 8, 0, 1), ("last", 0, 0, 1), ("last", 6, 0, 1), ("last", 4, 0, 1), ("last", 5, 0, 1), ("last", 3, 0, 1), ("row", "own", 1), ("end", 0, 0, 1), ("end", 1, 0, 1), ("end", 2, 0, 1), ("end", 3, 0, 1), ("end", 4, 0, 1), ("end", 5, 0, 1), ("end", 6, 0, 1), ("end", 7, 0, 1), ("end", 8, 0, 1), ("results",), ("row", "end", 0), ("row", "end", 1)],
     },
 }
-SMALL_UNITS = [Unit(0, (0, 384), (0, 128), "R", 0), Unit(0, (384, 512), (0, 128), "P", 0)]
-SMALL_PLAN = [("begin", 0, 0, 8), ("begin", 1, 0, 8), ("core", 1, 0, 8), ("core", 0, 0, 8), ("x", 0, 0, 4), ("y", 1, 0, 8), ("own", 0, 0, 1), ("x", 1, 0, 4),
+SMALL_UNITS = [Unit(0, (0, 256), (0, 128), "R", 0), Unit(0, (256, 640), (0, 128), "P", 0)]
+SMALL_PLAN = [("begin", 0, 0, 8), ("begin", 1, 0, 8), ("core", 1, 0, 4), ("core", 0, 0, 4), ("core", 1, 4, 4), ("core", 0, 4, 4), ("y", 1, 0, 4), ("x", 0, 0, 4), ("y", 1, 4, 4), ("x", 1, 0, 4), ("own", 0, 0, 1),
               ("last", 0, 0, 1), ("own", 1, 0, 1), ("last", 1, 0, 1), ("end", 0, 0, 1), ("end", 1, 0, 1)]
 
 

time: 321 us -> 321 us (level)
  no operation moved by 1% of the time
where the time goes in v3:
time: 321 us; the launch traced here: 320 us
  Pallas kernels  318 us (99%)
    pallas_call x1, Pallas kernels, backward(): pl.pallas_call(functools.partial(back_kernel, span, min(512, nk), units,...  155 us
    pallas_call x1, Pallas kernels, forward(): pl.pallas_call(functools.partial(forward_kernel, span, chunk, units, narr...  124 us
    pallas_call x1, Pallas kernels, reduce_weights(): pl.pallas_call(functools.partial(reduce_kernel, units, narr, plan), out_s...  24.7 us
    pallas_call x1, Pallas kernels, products(): pl.pallas_call(products_kernel, grid=(rows,), out_shape=[sd(tokens.shape,...  7.77 us

profile of v3, /device:TPU:0, one launch (start us, length us, event | category | flops | bytes accessed | tf_op | source)
XLA Modules:
  0.0 320.3 jit_solution(11993109138214830708)
XLA Ops:
  0.6 0.6 multiply_exponential_fusion.inverse
  1.3 2.3 prepare.1
  3.6 124.3 %forward.1 = (bf16[2,256,1024]{2,1,0:T(8,128)(2,1)}, f32[2,8,12,256]{3,2,1,0:T(8,128)}, f32[2,384,256]{2,1,0:T(8,128)}, bf16[8,2,320,256]{3,2,1,0:T(8,128)(2,1)}...) custom-call(bf16[2,256,1024]{2,1,0:T(8,128)(2,1)} %tok_ref.3, ...), custom_call_target="tpu_custom_call" | custom-call | tf_op jit(solution)/shard_map/forward/pallas_call | solution.py:1118
  127.9 154.6 %backward.1 = (f32[2,8,12,256]{3,2,1,0:T(8,128)}, f32[2,384,256]{2,1,0:T(8,128)}, bf16[2,320,256]{2,1,0:T(8,128)(2,1)}, bf16[2,256,1024]{2,1,0:T(8,128)(2,1)}, f...) custom-call(f32[2,8,12,256]{3,2,1,0:T(8,128)} %get-tuple-element.62., ...), custom_call_target="tpu_custom_call" | custom-call | tf_op jit(solution)/shard_map/backward/pallas_call | solution.py:867
  282.4 7.8 %products.1 = (f32[2,256,1024]{2,1,0:T(8,128)}, bf16[8,896,128]{2,1,0:T(8,128)(2,1)}) custom-call(f32[2,8,12,256]{3,2,1,0:T(8,128)} %get-tuple-element.73.dqh_ref, f32[2,384,256]{2,1,0:T(8,128)} %get-tuple-element.74.dqr_ref, bf16[2,320,256]{2,1,0:T(8,128)(2,1)} %get-tuple-element.75.mine_ref, f32[32,256]{1,0:T(8,128)} %get-tuple-element.56.cos_ref, ...), custom_call_target="tpu_custom_call" | custom-call | tf_op jit(solution)/shard_map/products/pallas_call | solution.py:1169
  290.2 0.0 copy-start
  290.2 24.7 %reduce_weights.1.small_ref = bf16[896,128]{1,0:T(8,128)(2,1)} custom-call(bf16[8,896,128]{2,1,0:T(8,128)(2,1)} %get-tuple-element.81.refs_0_), custom_call_target="tpu_custom_call" | custom-call | tf_op jit(solution)/shard_map/reduce_weights/pallas_call | solution.py:248
  314.9 4.4 %results.1 = (f32[96,128]{1,0:T(8,128)}, f32[128,384]{1,0:T(8,128)}, f32[32,128]{1,0:T(8,128)}, f32[128,128]{1,0:T(8,128)}, f32[32,128]{1,0:T(8,128)}, /*index=5...) custom-call(bf16[896,128]{1,0:T(8,128)(2,1)} %reduce_weights.1.small, ...), custom_call_target="tpu_custom_call" | custom-call | tf_op jit(solution)/shard_map/results/pallas_call | solution.py:1210
  319.4 0.0 copy-done
  319.4 1.0 copy.31
Async XLA Ops:
  290.2 29.1 %copy-start = (bf16[2,256,1024]{2,1,0:T(8,128)(2,1)S(1)}, bf16[2,256,1024]{2,1,0:T(8,128)(2,1)}, u32[]{:S(2)}) copy-start(bf16[2,256,1024]{2,1,0:T(8,128)(2,1)} %get-tuple-element.112) | copy-start | bytes 3145732
